TPU v7x, 32 devices: a whole 2x2x4 slice. The times are simulated.
32 devices in a mesh: frames: 8 (over z, core), rows: 4 (over y, x).
Axes of the slice: x: 2, y: 2, z: 4, core: 2. Of those that a mesh axis runs over, the one named last changes fastest.
Arguments:
- images: float32 [16, 8, 96, 128], P('frames', 'rows'), may hold values from -6 to 6
- spatial_weight: float32 [3, 3, 128, 128], replicated, may hold values from -0.1875 to 0.1875
- temporal_weight: float32 [3, 128, 128], replicated, may hold values from -0.3125 to 0.3125
- cotangent: float32 [16, 8, 96, 128], P('frames', 'rows'), may hold values from -6 to 6
Outputs:
- block_out: float32 [16, 8, 96, 128], P('frames', 'rows')
- grad_images: float32 [16, 8, 96, 128], P('frames', 'rows')
- grad_spatial: float32 [3, 3, 128, 128], P(None, None, None, 'rows')
- grad_temporal: float32 [3, 128, 128], P(None, None, 'rows')
All inputs are finite; a program needn't handle non-finite values.
Results may differ from a plain program's by a relative error of at most 0.0003.
Values sent between devices are 32-bit elements; how exact they have to be, the bound alone decides.
A program may use at most 64 MiB of HBM per device.

v0:
```python
import math

import jax
import jax.numpy as jnp
from jax import lax
from jax.sharding import PartitionSpec as P

HIGH = lax.Precision.HIGHEST


def padded_2(value, sides, width):
    for axis, dim in sides:
        count, length = (lax.axis_size(axis), value.shape[dim])
        up = [(i, (i + 1) % count) for i in range(count - 1)]
        down = [(j, i) for i, j in up]
        last = lax.slice_in_dim(value, length - width, length, axis=dim)
        leading = lax.slice_in_dim(value, 0, width, axis=dim)
        before = lax.ppermute(last, axis, up)
        after = lax.ppermute(leading, axis, down)
        value = jnp.concatenate([before, value, after], axis=dim)
    return value


def passed_along(value, axis, by):
    count = lax.axis_size(axis)
    pairs = [(i, i + by) for i in range(count) if 0 <= i + by < count]
    return lax.ppermute(value, axis, pairs)


def widen(array):
    return jnp.pad(array, ((0, 0), (0, 0), (1, 1), (0, 0)))


def convolve(source, kernel, height, width):
    total = jnp.zeros((source.shape[0], height, width, kernel.shape[3]), jnp.float32)
    for i in range(3):
        for j in range(3):
            total = total + jnp.einsum(
                "frwc,cd->frwd",
                source[:, i : i + height, j : j + width],
                kernel[i, j],
                precision=HIGH,
            )
    return total


def temporal_back(grad_long, temporal_weight, nframes):
    dact = jnp.zeros((nframes,) + grad_long.shape[1:], jnp.float32)
    for k in range(3):
        dact = dact + jnp.einsum(
            "frwd,cd->frwc", grad_long[k : k + nframes], temporal_weight[k], precision=HIGH
        )
    return dact


def per_device(images, spatial_weight, temporal_weight, cotangent):
    nframes, strip, width, chans = images.shape
    padded = widen(padded_2(images, (("rows", 1),), 1))
    pre = convolve(padded, spatial_weight, strip, width)
    sig = jax.nn.sigmoid(pre)
    later = passed_along(cotangent, "frames", -1)
    grad_long = jnp.concatenate([cotangent, later], axis=0)
    dact = temporal_back(grad_long, temporal_weight, nframes)
    dpre = dact * sig * (1.0 + pre * (1.0 - sig))
    dpre_wide = widen(padded_2(dpre, (("rows", 1),), 1))
    act = pre * sig
    earlier = passed_along(act, "frames", 1)
    longer = jnp.concatenate([earlier, act], axis=0)
    mixed = jnp.zeros(images.shape, jnp.float32)
    for k in range(3):
        mixed = mixed + jnp.einsum(
            "frwc,cd->frwd", longer[2 - k : 2 - k + nframes], temporal_weight[k], precision=HIGH
        )
    block_out = images + mixed
    grad_images = cotangent
    for i in range(3):
        for j in range(3):
            grad_images = grad_images + jnp.einsum(
                "frwd,cd->frwc",
                dpre_wide[:, 2 - i : 2 - i + strip, 2 - j : 2 - j + width],
                spatial_weight[i, j],
                precision=HIGH,
            )
    total_cells = nframes * lax.axis_size("frames") * strip * lax.axis_size("rows") * width
    factor = 1.0 / math.sqrt(total_cells)
    rows_out = []
    for i in range(3):
        cols_out = []
        for j in range(3):
            cols_out.append(
                jnp.einsum(
                    "frwc,frwd->cd", padded[:, i : i + strip, j : j + width], dpre, precision=HIGH
                )
            )
        rows_out.append(jnp.stack(cols_out))
    spatial_terms = jnp.stack(rows_out).reshape(9, chans, chans) * factor
    temporal_terms = (
        jnp.stack(
            [
                jnp.einsum(
                    "frwc,frwd->cd", longer[2 - k : 2 - k + nframes], cotangent, precision=HIGH
                )
                for k in range(3)
            ]
        )
        * factor
    )
    all_terms = jnp.concatenate([spatial_terms, temporal_terms], axis=0)
    shares = lax.psum_scatter(all_terms, "rows", scatter_dimension=2, tiled=True)
    summed = lax.psum(shares, "frames")
    grad_spatial = summed[:9].reshape(3, 3, chans, summed.shape[2])
    grad_temporal = summed[9:]
    return (block_out, grad_images, grad_spatial, grad_temporal)


def solution(mesh):
    return jax.shard_map(
        per_device,
        mesh=mesh,
        in_specs=(P("frames", "rows", None, None), P(), P(), P("frames", "rows", None, None)),
        out_specs=(
            P("frames", "rows", None, None),
            P("frames", "rows", None, None),
            P(None, None, None, "rows"),
            P(None, None, "rows"),
        ),
        check_vma=False,
    )
```

profile of v0, /device:TPU:0, one launch (start us, length us, event | category | flops | bytes accessed | tf_op | source)
XLA Modules:
  0.0 141.2 jit_solution(2839915301673886561)
XLA Ops:
  7.2 1.1 fusion.109
  8.3 4.8 %collective-permute-start = (f32[2,1,96,128]{3,2,1,0:T(8,128)S(1)}, f32[2,1,96,128]{3,2,1,0:T(8,128)S(1)}, u32[]{:S(2)}, u32[]{:S(2)}) collective-permute-start(f32[2,1,96,128]{3,2,1,0:T(8,128)S(1)} %get-tuple-element.8), channel_id=1, source_target_pairs={{0,1},{1,2},{2,3},{4,5},{5,6},{6,7},{8,9},{9,10},{10,11},{12,13},{... | collective-permute-start | bytes 294920 | tf_op jit(solution)/shard_map/ppermute | solution.py:18
  13.2 1.3 collective-permute-start.1
  14.5 1.3 collective-permute-start.3
  16.2 0.9 copy-done
  17.6 2.1 %collective-permute-done.1 = f32[2,1,96,128]{3,2,1,0:T(8,128)S(1)} collective-permute-done((f32[2,1,96,128]{3,2,1,0:T(8,128)S(1)}, f32[2,1,96,128]{3,2,1,0:T(8,128)S(1)}, u32[]{:S(2)}, u32[]{:S(2)}) %collective-permute-start.1) | collective-permute-done | bytes 98336 | tf_op jit(solution)/shard_map/ppermute | solution.py:19
  22.8 1.3 collective-permute-start.2
  24.1 1.0 fusion.75
  30.7 4.3 %collective-permute-start.4 = (f32[2,1,96,128]{3,2,1,0:T(8,128)S(1)}, f32[2,1,96,128]{3,2,1,0:T(8,128)S(1)}, u32[]{:S(2)}, u32[]{:S(2)}) collective-permute-start(f32[2,1,96,128]{3,2,1,0:T(8,128)S(1)} %get-tuple-element.4), channel_id=1, source_target_pairs={{0,1},{1,2},{2,3},{4,5},{5,6},{6,7},{8,9},{9,10},{10,11},{12,13},{... | collective-permute-start | bytes 294920 | tf_op jit(solution)/shard_map/ppermute | solution.py:18
  35.0 1.3 collective-permute-start.5
  36.7 0.5 collective-permute-done.4
  37.2 5.5 %collective-permute-done.5 = f32[2,1,96,128]{3,2,1,0:T(8,128)} collective-permute-done((f32[2,1,96,128]{3,2,1,0:T(8,128)S(1)}, f32[2,1,96,128]{3,2,1,0:T(8,128)}, u32[]{:S(2)}, u32[]{:S(2)}) %collective-permute-start.5) | collective-permute-done | bytes 98336 | tf_op jit(solution)/shard_map/ppermute | solution.py:19
  42.7 0.9 select_maximum_fusion
  43.9 1.0 fusion.26
  46.1 1.0 pad_maximum_fusion
  48.3 0.6 copy-done.5
  49.6 0.6 copy-done.6
  50.2 1.0 fusion.8
  51.2 1.3 fusion.11
  52.4 21.9 %reduce-scatter.2.cloned.1.call-done = f32[12,128,32]{1,2,0:T(8,128)} async-done(((f32[12,128,128]{1,2,0:T(8,128)}), f32[12,128,32]{1,2,0:T(8,128)}) %reduce-scatter.2.cloned.1.call-update) | async-done | bytes 196624 | tf_op jit(solution)/shard_map/reduce_scatter | solution.py:109
  74.4 1.0 fusion
  75.4 55.9 %all-reduce.4.cloned.1.call-done = f32[12,128,32]{1,2,0:T(8,128)} async-done(((f32[12,128,32]{1,2,0:T(8,128)}), f32[12,128,32]{1,2,0:T(8,128)}) %all-reduce.4.cloned.1.call-update) | async-done | bytes 196624 | tf_op jit(solution)/shard_map/psum | solution.py:110
  131.3 1.4 %slice.193 = f32[3,128,32]{1,2,0:T(8,128)} slice(f32[12,128,32]{1,2,0:T(8,128)} %all-reduce.4.cloned.1.call-done), slice={[9:12], [0:128], [0:32]} | slice | bytes 98304 | tf_op jit(solution)/shard_map/slice | solution.py:112
  132.7 1.6 %slice.192 = f32[9,128,32]{1,2,0:T(8,128)} slice(f32[12,128,32]{1,2,0:T(8,128)} %all-reduce.4.cloned.1.call-done), slice={[0:9], [0:128], [0:32]} | slice | bytes 294912 | tf_op jit(solution)/shard_map/slice | solution.py:111
  (60 shorter events, 13.2 us)
Async XLA Ops:
  7.2 7.3 %copy-start.1 = (f32[2,2,96,128]{3,2,1,0:T(8,128)S(1)}, f32[2,2,96,128]{3,2,1,0:T(8,128)}, u32[]{:S(2)}) copy-start(f32[2,2,96,128]{3,2,1,0:T(8,128)} %param.7) | copy-start | bytes 589828
  7.2 8.6 %copy-start.4 = (f32[3,128,128]{2,1,0:T(8,128)S(1)}, f32[3,128,128]{2,1,0:T(8,128)}, u32[]{:S(2)}) copy-start(f32[3,128,128]{2,1,0:T(8,128)} %param.6) | copy-start | bytes 589828
  7.2 67.2 %reduce-scatter.2.cloned.1.call-start = ((), (), s32[]{:S(2)}) async-start(), calls=%async_computation.1 | async-start | bytes 983040 | tf_op jit(solution)/shard_map/reduce_scatter | solution.py:109
  8.3 7.8 %collective-permute-start = (f32[2,1,96,128]{3,2,1,0:T(8,128)S(1)}, f32[2,1,96,128]{3,2,1,0:T(8,128)S(1)}, u32[]{:S(2)}, u32[]{:S(2)}) collective-permute-start(f32[2,1,96,128]{3,2,1,0:T(8,128)S(1)} %get-tuple-element.8), channel_id=1, source_target_pairs={{0,1},{1,2},{2,3},{4,5},{5,6},{6,7},{8,9},{9,10},{10,11},{12,13},{... | collective-permute-start | bytes 294920 | tf_op jit(solution)/shard_map/ppermute | solution.py:18
  13.2 6.5 %collective-permute-start.1 = (f32[2,1,96,128]{3,2,1,0:T(8,128)S(1)}, f32[2,1,96,128]{3,2,1,0:T(8,128)S(1)}, u32[]{:S(2)}, u32[]{:S(2)}) collective-permute-start(f32[2,1,96,128]{3,2,1,0:T(8,128)S(1)} %get-tuple-element.9), channel_id=1, source_target_pairs={{1,0},{2,1},{3,2},{5,4},{6,5},{7,6},{9,8},{10,9},{11,10},{13,12},{... | collective-permute-start | bytes 294920 | tf_op jit(solution)/shard_map/ppermute | solution.py:19
  14.5 10.7 %collective-permute-start.3 = (f32[2,2,96,128]{3,2,1,0:T(8,128)S(1)}, f32[2,2,96,128]{3,2,1,0:T(8,128)S(1)}, u32[]{:S(2)}, u32[]{:S(2)}) collective-permute-start(f32[2,2,96,128]{3,2,1,0:T(8,128)S(1)} %copy-done.1), channel_id=1, source_target_pairs={{4,0},{8,4},{12,8},{16,12},{20,16},{24,20},{28,24},{5,1},{9,5},{13... | collective-permute-start | bytes 589832 | tf_op jit(solution)/shard_map/ppermute | solution.py:27
  16.1 0.9 copy-start
  16.1 1.2 copy-start.2
  22.8 22.1 %collective-permute-start.2 = (f32[2,2,96,128]{3,2,1,0:T(8,128)S(1)}, f32[2,2,96,128]{3,2,1,0:T(8,128)S(1)}, u32[]{:S(2)}, u32[]{:S(2)}) collective-permute-start(f32[2,2,96,128]{3,2,1,0:T(8,128)S(1)} %get-tuple-element.10), channel_id=1, source_target_pairs={{0,4},{4,8},{8,12},{12,16},{16,20},{20,24},{24,28},{1,5},{5,9},{9,... | collective-permute-start | bytes 589832 | tf_op jit(solution)/shard_map/ppermute | solution.py:27
  30.7 6.5 %collective-permute-start.4 = (f32[2,1,96,128]{3,2,1,0:T(8,128)S(1)}, f32[2,1,96,128]{3,2,1,0:T(8,128)S(1)}, u32[]{:S(2)}, u32[]{:S(2)}) collective-permute-start(f32[2,1,96,128]{3,2,1,0:T(8,128)S(1)} %get-tuple-element.4), channel_id=1, source_target_pairs={{0,1},{1,2},{2,3},{4,5},{5,6},{6,7},{8,9},{9,10},{10,11},{12,13},{... | collective-permute-start | bytes 294920 | tf_op jit(solution)/shard_map/ppermute | solution.py:18
  35.0 7.6 %collective-permute-start.5 = (f32[2,1,96,128]{3,2,1,0:T(8,128)S(1)}, f32[2,1,96,128]{3,2,1,0:T(8,128)}, u32[]{:S(2)}, u32[]{:S(2)}) collective-permute-start(f32[2,1,96,128]{3,2,1,0:T(8,128)S(1)} %get-tuple-element.5), channel_id=1, source_target_pairs={{1,0},{2,1},{3,2},{5,4},{6,5},{7,6},{9,8},{10,9},{11,10},{13,12},{... | collective-permute-start | bytes 294920 | tf_op jit(solution)/shard_map/ppermute | solution.py:19
  47.1 84.2 %all-reduce.4.cloned.1.call-start = ((), (), s32[]{:S(2)}) async-start(), calls=%async_computation.2 | async-start | bytes 393216 | tf_op jit(solution)/shard_map/psum | solution.py:110
  48.0 0.9 copy-start.5
  49.2 0.9 copy-start.6
  50.2 1.0 copy-start.3
Sparse Core Ops, SparseCore 0:
  47.2 27.1 reduce-scatter.1
  76.7 54.5 all-reduce.3
where the time goes:
time: 142 us; the launch traced here: 141 us
  waiting for transfers between devices  85.9 us (60%)
  matrix products  17.3 us (12%)
  starting transfers between devices  14.6 us (10%)
  between operations  14.5 us (10%)
  local copies, waits for them, and re-layouts  6.77 us (5%)
  other arithmetic  2.05 us (1%)
    psum x1, waiting for transfers between devices, per_device(): summed = lax.psum(shares, 'frames')  55.9 us
    reduce_scatter x1, waiting for transfers between devices, per_device(): lax.psum_scatter(all_terms, 'rows', scatter_dimension=2, tiled=True)  21.9 us
    ppermute x2, starting transfers between devices, padded_2(): before = lax.ppermute(last, axis, up)  9.15 us
    ppermute x2, waiting for transfers between devices, padded_2(): after = lax.ppermute(leading, axis, down)  7.52 us
    dot_general x9, matrix products, per_device(): jnp.einsum('frwd,cd->frwc', dpre_wide[:, 2 - i:2 - i + strip, 2 - j:2 - j...  5.25 us
    dot_general x9, matrix products, per_device(): jnp.einsum('frwc,frwd->cd', padded[:, i:i + strip, j:j + width], dpre, pr...  4.45 us
  transfers between devices with their start and end apart: 8, of which 5 were waited for; matrix products, arithmetic and copies ran while one was open for 13% of the time, Pallas kernels for 0%

commit v1 on v0

v1 whole, which is shorter than its diff:
```python
import functools
import math

import jax
import jax.numpy as jnp
from jax import lax
from jax.experimental import pallas as pl
from jax.experimental.pallas import tpu as pltpu
from jax.sharding import PartitionSpec as P

MESH = pl.DeviceIdType.MESH
F32, BF16 = jnp.float32, jnp.bfloat16
GROUPS = 2


def split(value):
    high = value.astype(BF16)
    return high, (value - high.astype(F32)).astype(BF16)


def dot(a, b):
    return jnp.dot(a, b, preferred_element_type=F32)


def put_weight(dst, index, value):
    high, low = split(value)
    n = value.shape[1]
    dst[index, :, :n] = high
    dst[index, :, n:] = low


def product(high, low, both):
    n = both.shape[1] // 2
    wide = dot(high, both)
    return wide[:, :n] + wide[:, n:] + dot(low, both[:, :n])


def put_row(dst, row, frames):
    width, chans = frames[0].shape
    at = lax.broadcasted_iota(jnp.int32, (width, chans), 0)
    for f, value in enumerate(frames):
        before = jnp.where(at == 0, 0.0, pltpu.roll(value, 1, 0))
        after = jnp.where(at == width - 1, 0.0, pltpu.roll(value, width - 1, 0))
        rows = pl.ds(f * width, width)
        for b, moved in enumerate((before, value, after)):
            high, low = split(moved)
            dst[row, rows, b * chans : (b + 1) * chans] = high
            dst[row, rows, (3 + b) * chans : (4 + b) * chans] = low


def kernel(
    nfd, nrd, share, piece, factor,
    x_ref, sw_ref, tw_ref, cot_ref, mix_ref, gi_ref, gr_ref,
    xs, ds, wf, wb, tf, tb, xhalo, chalo, ahalo, dhalo, act, dpre, cots, acts,
    terms, core_in, half, rows_in, plane, z_in, own, final, send_sem, recv_sem,
):
    nf, strip, width, chans = x_ref.shape
    assert nf == 2 and strip == 2
    wide = nf * width
    three = 3 * chans
    fr, ro = lax.axis_index("frames"), lax.axis_index("rows")
    core, z = lax.rem(fr, 2), lax.div(fr, 2)
    nz = nfd // 2
    other = fr + 1 - 2 * core
    n_sems = [0]
    sent = []

    def remote(src, dst, **where):
        n = n_sems[0]
        n_sems[0] += 1
        return pltpu.make_async_remote_copy(
            src_ref=src, dst_ref=dst, send_sem=send_sem.at[n], recv_sem=recv_sem.at[n],
            device_id=where, device_id_type=MESH,
        )

    def send(src, dst, **where):
        copy = remote(src, dst, **where)
        copy.start()
        sent.append(copy)
        return copy

    barrier = pltpu.get_barrier_semaphore()
    for o in range(1, nrd):
        pl.semaphore_signal(barrier, inc=1, device_id={"rows": lax.rem(ro + o, nrd)}, device_id_type=MESH)
    for o in range(1, nfd):
        pl.semaphore_signal(barrier, inc=1, device_id={"frames": lax.rem(fr + o, nfd)}, device_id_type=MESH)

    for h in range(strip):
        put_row(xs, h + 1, [x_ref[f, h] for f in range(nf)])

    pl.semaphore_wait(barrier, nrd - 1 + nfd - 1)

    has_up, has_down = ro > 0, ro < nrd - 1
    has_prev, has_next = fr > 0, fr < nfd - 1
    up, down = lax.rem(ro + nrd - 1, nrd), lax.rem(ro + 1, nrd)
    prev, following = lax.rem(fr + nfd - 1, nfd), lax.rem(fr + 1, nfd)
    x_up = remote(x_ref.at[:, 0], xhalo.at[1], rows=up)
    x_down = remote(x_ref.at[:, strip - 1], xhalo.at[0], rows=down)
    c_prev = remote(cot_ref, chalo, frames=prev)
    a_next = remote(act, ahalo, frames=following)
    d_up = remote(dpre.at[0], dhalo.at[1], rows=up)
    d_down = remote(dpre.at[strip - 1], dhalo.at[0], rows=down)

    def receive(copy, there, zeroed):
        @pl.when(there)
        def _():
            copy.wait_recv()

        @pl.when(jnp.logical_not(there))
        def _():
            zeroed[...] = jnp.zeros(zeroed.shape, F32)

    @pl.when(has_up)
    def _():
        x_up.start()

    @pl.when(has_down)
    def _():
        x_down.start()

    @pl.when(has_prev)
    def _():
        c_prev.start()

    for i in range(3):
        put_weight(wf, i, sw_ref[i].reshape(three, chans))
    for k in range(3):
        put_weight(tb, k, tw_ref[k].T)
        put_weight(tf, k, tw_ref[k])
    for f in range(nf):
        for h in range(strip):
            high, low = split(cot_ref[f, h])
            cots[0, h, pl.ds(f * width, width), :] = high
            cots[1, h, pl.ds(f * width, width), :] = low

    def conv(src, row, weight, i):
        return product(src[row, :, :three], src[row, :, three:], weight[i])

    pre = [conv(xs, 1, wf, 1) + conv(xs, 2, wf, 2), conv(xs, 1, wf, 0) + conv(xs, 2, wf, 1)]
    for i in range(3):
        put_weight(wb, i, jnp.concatenate([sw_ref[i, 2 - b].T for b in range(3)], axis=0))

    receive(x_down, has_up, xhalo.at[0])
    receive(x_up, has_down, xhalo.at[1])
    put_row(xs, 0, [xhalo[0, f] for f in range(nf)])
    put_row(xs, 3, [xhalo[1, f] for f in range(nf)])
    pre = [pre[0] + conv(xs, 0, wf, 0), pre[1] + conv(xs, 3, wf, 2)]
    receive(c_prev, has_next, chalo)
    for f in range(nf):
        for h in range(strip):
            high, low = split(chalo[f, h])
            cots[0, h, pl.ds(wide + f * width, width), :] = high
            cots[1, h, pl.ds(wide + f * width, width), :] = low

    both_act, both_dpre = [], []
    for h in range(strip):
        sig = 1.0 / (1.0 + jnp.exp(-pre[h]))
        act_h = pre[h] * sig
        act[h] = act_h
        dact = None
        for k in range(3):
            rows = pl.ds(k * width, wide)
            term = product(cots[0, h, rows, :], cots[1, h, rows, :], tb[k])
            dact = term if dact is None else dact + term
        dpre_h = dact * sig * (1.0 + pre[h] * (1.0 - sig))
        dpre[h] = dpre_h
        both_act.append(act_h)
        both_dpre.append(dpre_h)

    @pl.when(has_up)
    def _():
        d_up.start()

    @pl.when(has_down)
    def _():
        d_down.start()

    @pl.when(has_next)
    def _():
        a_next.start()

    act_t = split(jnp.concatenate(both_act, axis=0).T)
    for k in range(3):
        rows = pl.ds(k * width, wide)
        c_high = cots[0, :, rows, :].reshape(strip * wide, chans)
        c_low = cots[1, :, rows, :].reshape(strip * wide, chans)
        term = dot(act_t[0], c_high) + dot(act_t[0], c_low) + dot(act_t[1], c_high)
        terms[0, 0, k] = term.T
    dpre_t = split(jnp.concatenate(both_dpre, axis=0).T)

    def spatial_terms(i, g, side):
        src = xs[i : i + strip].reshape(strip * wide, 2 * three)
        wide_term = dot(dpre_t[0], src)
        term = wide_term[:, :three] + wide_term[:, three:] + dot(dpre_t[1], src[:, :three])
        for j in range(3):
            terms[g, side, j] = term[:, j * chans : (j + 1) * chans]

    spatial_terms(0, 0, 1)
    to_core = [None] * GROUPS
    to_rows = [None] * GROUPS
    to_z = [None] * GROUPS
    around_z = [None] * GROUPS
    back = [None] * GROUPS

    def start_core(g):
        to_core[g] = send(terms.at[g, 1 - core], core_in.at[g], frames=other)

    def start_rows(g):
        to_core[g].wait_recv()
        half[g] = terms[g, core] + core_in[g]
        to_rows[g] = []
        for o in range(1, nrd):
            target = lax.rem(ro + o, nrd)
            part = pl.ds(pl.multiple_of(target * share, 8), share)
            to_rows[g].append(send(half.at[g, :, part, :], rows_in.at[g, o - 1], rows=target))

    def start_z(g):
        total = half[g, :, pl.ds(pl.multiple_of(ro * share, 8), share), :]
        for o in range(1, nrd):
            to_rows[g][o - 1].wait_recv()
            total = total + rows_in[g, o - 1]
        plane[g, : 3 * share] = total.reshape(3 * share, chans) * factor
        if nz * piece > 3 * share:
            plane[g, 3 * share :] = jnp.zeros((nz * piece - 3 * share, chans), F32)
        to_z[g] = []
        for o in range(1, nz):
            target = lax.rem(z + o, nz)
            part = pl.ds(pl.multiple_of(target * piece, 8), piece)
            to_z[g].append(send(plane.at[g, part], z_in.at[g, o - 1], frames=2 * target + core))

    def start_around(g):
        mine = pl.ds(pl.multiple_of(z * piece, 8), piece)
        total = plane[g, mine]
        for o in range(1, nz):
            to_z[g][o - 1].wait_recv()
            total = total + z_in[g, o - 1]
        own[g, 0] = total
        final[g, core, mine] = total
        around_z[g] = []
        for o in range(1, nz):
            target = lax.rem(z + o, nz)
            around_z[g].append(send(own.at[g, 0], final.at[g, core, mine], frames=2 * target + core))

    def start_back(g):
        for copy in around_z[g]:
            copy.wait_recv()
        back[g] = send(final.at[g, core], final.at[g, core], frames=other)

    def finish(g):
        back[g].wait_recv()
        gr_ref[g] = final[g]

    def mixed():
        receive(a_next, has_prev, ahalo)
        for h in range(strip):
            for part, value in ((0, ahalo[h]), (1, act[h])):
                high, low = split(value)
                acts[0, h, pl.ds(part * wide, wide), :] = high
                acts[1, h, pl.ds(part * wide, wide), :] = low
        for h in range(strip):
            total = None
            for k in range(3):
                rows = pl.ds((2 - k) * width, wide)
                term = product(acts[0, h, rows, :], acts[1, h, rows, :], tf[k])
                total = term if total is None else total + term
            for f in range(nf):
                mix_ref[f, h] = total[f * width : (f + 1) * width]

    def image_gradient():
        receive(d_down, has_up, dhalo.at[0])
        receive(d_up, has_down, dhalo.at[1])
        put_row(ds, 0, [dhalo[0, pl.ds(f * width, width)] for f in range(nf)])
        put_row(ds, 3, [dhalo[1, pl.ds(f * width, width)] for f in range(nf)])
        for h in range(strip):
            put_row(ds, h + 1, [dpre[h, pl.ds(f * width, width)] for f in range(nf)])
        for h in range(strip):
            total = conv(ds, h + 2, wb, 0) + conv(ds, h + 1, wb, 1) + conv(ds, h, wb, 2)
            for f in range(nf):
                gi_ref[f, h] = total[f * width : (f + 1) * width]

    start_core(0)
    spatial_terms(1, 1, 0)
    spatial_terms(2, 1, 1)
    start_core(1)
    start_rows(0)
    start_rows(1)
    mixed()
    start_z(0)
    image_gradient()
    start_z(1)
    start_around(0)
    start_around(1)
    start_back(0)
    start_back(1)
    finish(0)
    finish(1)

    for copy in sent:
        copy.wait_send()
    for copy, there in (
        (x_up, has_up), (x_down, has_down), (c_prev, has_prev),
        (a_next, has_next), (d_up, has_up), (d_down, has_down),
    ):
        pl.when(there)(copy.wait_send)


def per_device(nfd, nrd, images, spatial_weight, temporal_weight, cotangent):
    nf, strip, width, chans = images.shape
    wide, three = nf * width, 3 * chans
    nz, share = nfd // 2, chans // nrd
    piece = -(-(3 * share) // nz)
    piece = -(-piece // 8) * 8
    factor = 1.0 / math.sqrt(nf * nfd * strip * nrd * width)
    n_sems = 6 + GROUPS * (2 + (nrd - 1) + 2 * (nz - 1))
    vmem = pl.BlockSpec(memory_space=pltpu.VMEM)
    mixed, gradient, grads = pl.pallas_call(
        functools.partial(kernel, nfd, nrd, share, piece, factor),
        out_shape=(
            jax.ShapeDtypeStruct(images.shape, F32),
            jax.ShapeDtypeStruct(images.shape, F32),
            jax.ShapeDtypeStruct((GROUPS, 2, nz * piece, chans), F32),
        ),
        in_specs=[vmem] * 4,
        out_specs=(vmem,) * 3,
        scratch_shapes=[
            pltpu.VMEM((strip + 2, wide, 2 * three), BF16),
            pltpu.VMEM((strip + 2, wide, 2 * three), BF16),
            pltpu.VMEM((3, three, 2 * chans), BF16),
            pltpu.VMEM((3, three, 2 * chans), BF16),
            pltpu.VMEM((3, chans, 2 * chans), BF16),
            pltpu.VMEM((3, chans, 2 * chans), BF16),
            pltpu.VMEM((2, nf, width, chans), F32),
            pltpu.VMEM((nf, strip, width, chans), F32),
            pltpu.VMEM((strip, wide, chans), F32),
            pltpu.VMEM((2, wide, chans), F32),
            pltpu.VMEM((strip, wide, chans), F32),
            pltpu.VMEM((strip, wide, chans), F32),
            pltpu.VMEM((2, strip, 2 * wide, chans), BF16),
            pltpu.VMEM((2, strip, 2 * wide, chans), BF16),
            pltpu.VMEM((GROUPS, 2, 3, chans, chans), F32),
            pltpu.VMEM((GROUPS, 3, chans, chans), F32),
            pltpu.VMEM((GROUPS, 3, chans, chans), F32),
            pltpu.VMEM((GROUPS, nrd - 1, 3, share, chans), F32),
            pltpu.VMEM((GROUPS, nz * piece, chans), F32),
            pltpu.VMEM((GROUPS, nz - 1, piece, chans), F32),
            pltpu.VMEM((GROUPS, 1, piece, chans), F32),
            pltpu.VMEM((GROUPS, 2, nz * piece, chans), F32),
            pltpu.SemaphoreType.DMA((n_sems,)),
            pltpu.SemaphoreType.DMA((n_sems,)),
        ],
        compiler_params=pltpu.CompilerParams(
            collective_id=0, has_side_effects=True, vmem_limit_bytes=24 * 2**20
        ),
        cost_estimate=pl.CostEstimate(flops=1_400_000_000, bytes_accessed=2_000_000, transcendentals=50_000),
    )(images, spatial_weight, temporal_weight, cotangent)
    grads = grads[:, :, : 3 * share].reshape(GROUPS * 2, 3, share, chans).transpose(0, 1, 3, 2)
    return images + mixed, cotangent + gradient, grads[1:], grads[0]


def solution(mesh):
    return jax.shard_map(
        functools.partial(per_device, mesh.shape["frames"], mesh.shape["rows"]),
        mesh=mesh,
        in_specs=(P("frames", "rows", None, None), P(), P(), P("frames", "rows", None, None)),
        out_specs=(
            P("frames", "rows", None, None),
            P("frames", "rows", None, None),
            P(None, None, None, "rows"),
            P(None, None, "rows"),
        ),
        check_vma=False,
    )
```

time: 142 us -> 38.4 us (0.27)
  the two profiles are of different devices: /device:TPU:0 before, /device:TPU:3 now
where the time goes in v1:
time: 38.4 us; the launch traced here: 38.2 us
  Pallas kernels  31 us (81%)
  local copies, waits for them, and re-layouts  5.13 us (13%)
  other arithmetic  1.4 us (4%)
  between operations  0.65 us (2%)
    pallas_call x1, Pallas kernels, per_device(): pl.pallas_call(functools.partial(kernel, nfd, nrd, share, piece, factor),...  31 us
    unnamed x8, local copies, waits for them, and re-layouts  3.84 us
    add x2, other arithmetic, per_device(): return (images + mixed, cotangent + gradient, grads[1:], grads[0])  1.4 us

profile of v1, /device:TPU:3, one launch (start us, length us, event | category | flops | bytes accessed | tf_op | source)
XLA Modules:
  0.0 38.2 jit_solution(16734150489270281535)
XLA Ops:
  0.6 0.0 copy-start
  0.6 0.9 %copy-done = f32[2,2,96,128]{3,2,1,0:T(8,128)S(1)} copy-done((f32[2,2,96,128]{3,2,1,0:T(8,128)S(1)}, f32[2,2,96,128]{3,2,1,0:T(8,128)}, u32[]{:S(2)}) %copy-start) | copy-done | bytes 196632
  1.6 0.0 copy-start.1
  1.6 0.9 %copy-done.1 = f32[2,2,96,128]{3,2,1,0:T(8,128)S(1)} copy-done((f32[2,2,96,128]{3,2,1,0:T(8,128)S(1)}, f32[2,2,96,128]{3,2,1,0:T(8,128)}, u32[]{:S(2)}) %copy-start.1) | copy-done | bytes 196632
  2.5 0.0 copy-start.2
  2.5 1.1 %copy-done.2 = f32[3,3,128,128]{3,2,1,0:T(8,128)S(1)} copy-done((f32[3,3,128,128]{3,2,1,0:T(8,128)S(1)}, f32[3,3,128,128]{3,2,1,0:T(8,128)}, u32[]{:S(2)}) %copy-start.2) | copy-done | bytes 589848
  3.6 0.0 copy-start.3
  3.6 0.9 %copy-done.3 = f32[3,128,128]{2,1,0:T(8,128)S(1)} copy-done((f32[3,128,128]{2,1,0:T(8,128)S(1)}, f32[3,128,128]{2,1,0:T(8,128)}, u32[]{:S(2)}) %copy-start.3) | copy-done | bytes 196632
  4.5 31.0 %shard_map.75 = (f32[2,2,96,128]{3,2,1,0:T(8,128)S(1)}, f32[2,2,96,128]{3,2,1,0:T(8,128)S(1)}, f32[2,2,96,128]{3,2,1,0:T(8,128)S(1)}) custom-call(f32[2,2,96,128]{3,2,1,0:T(8,128)S(1)} %copy-done, f32[3,3,128,128]{3,2,1,0:T(8,128)S(1)} %copy-done.2, f32[3,128,128]{2,1,0:T(8,128)S(1)} %copy-done.3, f32[2,2,96,128]{3,2,1,0:T(8,128)S(1)} %copy-done.1), custom_call_target="tpu_custom_call" | custom-call | flops 1400000000 | bytes 2000000 | tf_op jit(solution)/shard_map/pallas_call | solution.py:316
  35.5 0.7 %add.6 = f32[2,2,96,128]{3,2,1,0:T(8,128)} add(f32[2,2,96,128]{3,2,1,0:T(8,128)S(1)} %copy-done, f32[2,2,96,128]{3,2,1,0:T(8,128)S(1)} %get-tuple-element.7) | non-fusion elementwise | flops 49152 | bytes 589824 | tf_op jit(solution)/shard_map/add | solution.py:357
  36.2 0.6 %slice_bitcast_fusion = f32[3,128,32]{1,2,0:T(8,128)} fusion(f32[4,3,128,32]{2,3,1,0:T(8,128)S(1)} %bitcast.5), kind=kLoop, calls=%fused_computation | loop fusion | bytes 98304 | tf_op jit(solution)/shard_map/squeeze | solution.py:357
  36.8 0.7 %slice.8 = f32[3,3,128,32]{2,3,1,0:T(8,128)} slice(f32[4,3,128,32]{2,3,1,0:T(8,128)S(1)} %bitcast.6), slice={[1:4], [0:3], [0:128], [0:32]} | slice | bytes 294912 | tf_op jit(solution)/shard_map/slice | solution.py:357
  37.5 0.7 %add.7 = f32[2,2,96,128]{3,2,1,0:T(8,128)} add(f32[2,2,96,128]{3,2,1,0:T(8,128)S(1)} %copy-done.1, f32[2,2,96,128]{3,2,1,0:T(8,128)S(1)} %get-tuple-element.8) | non-fusion elementwise | flops 49152 | bytes 589824 | tf_op jit(solution)/shard_map/add | solution.py:357
Async XLA Ops:
  0.6 0.9 %copy-start = (f32[2,2,96,128]{3,2,1,0:T(8,128)S(1)}, f32[2,2,96,128]{3,2,1,0:T(8,128)}, u32[]{:S(2)}) copy-start(f32[2,2,96,128]{3,2,1,0:T(8,128)} %x_ref.1) | copy-start | bytes 589828
  1.6 0.9 %copy-start.1 = (f32[2,2,96,128]{3,2,1,0:T(8,128)S(1)}, f32[2,2,96,128]{3,2,1,0:T(8,128)}, u32[]{:S(2)}) copy-start(f32[2,2,96,128]{3,2,1,0:T(8,128)} %cot_ref.1) | copy-start | bytes 589828
  2.5 1.1 %copy-start.2 = (f32[3,3,128,128]{3,2,1,0:T(8,128)S(1)}, f32[3,3,128,128]{3,2,1,0:T(8,128)}, u32[]{:S(2)}) copy-start(f32[3,3,128,128]{3,2,1,0:T(8,128)} %sw_ref.1) | copy-start | bytes 1769476
  3.6 0.9 %copy-start.3 = (f32[3,128,128]{2,1,0:T(8,128)S(1)}, f32[3,128,128]{2,1,0:T(8,128)}, u32[]{:S(2)}) copy-start(f32[3,128,128]{2,1,0:T(8,128)} %tw_ref.1) | copy-start | bytes 589828

commit v2 on v1

--- a/solution.py
+++ b/solution.py
@@ -11,6 +11,7 @@
 MESH = pl.DeviceIdType.MESH
 F32, BF16 = jnp.float32, jnp.bfloat16
 GROUPS = 2
+VMEM_LIMIT = 60 * 2**20
 
 
 def split(value):
@@ -50,8 +51,8 @@
 
 def kernel(
     nfd, nrd, share, piece, factor,
-    x_ref, sw_ref, tw_ref, cot_ref, mix_ref, gi_ref, gr_ref,
-    xs, ds, wf, wb, tf, tb, xhalo, chalo, ahalo, dhalo, act, dpre, cots, acts,
+    x_hbm, sw_hbm, tw_hbm, cot_hbm, mix_hbm, gi_hbm, gr_hbm,
+    x_ref, sw_ref, tw_ref, cot_ref, mix_ref, gi_ref, load_sem, store_sem, xs, ds, wf, wb, tf, tb, xhalo, chalo, ahalo, dhalo, act, dpre, cots, acts,
     terms, core_in, half, rows_in, plane, z_in, own, final, send_sem, recv_sem,
 ):
     nf, strip, width, chans = x_ref.shape
@@ -63,7 +64,7 @@
     nz = nfd // 2
     other = fr + 1 - 2 * core
     n_sems = [0]
-    sent = []
+    sent, stores = [], []
 
     def remote(src, dst, **where):
         n = n_sems[0]
@@ -79,14 +80,24 @@
         sent.append(copy)
         return copy
 
+    loads = [
+        pltpu.make_async_copy(src, dst, load_sem.at[n])
+        for n, (src, dst) in enumerate(
+            ((x_hbm, x_ref), (cot_hbm, cot_ref), (tw_hbm, tw_ref), (sw_hbm, sw_ref))
+        )
+    ]
+    for load in loads:
+        load.start()
     barrier = pltpu.get_barrier_semaphore()
     for o in range(1, nrd):
         pl.semaphore_signal(barrier, inc=1, device_id={"rows": lax.rem(ro + o, nrd)}, device_id_type=MESH)
     for o in range(1, nfd):
         pl.semaphore_signal(barrier, inc=1, device_id={"frames": lax.rem(fr + o, nfd)}, device_id_type=MESH)
 
+    loads[0].wait()
     for h in range(strip):
         put_row(xs, h + 1, [x_ref[f, h] for f in range(nf)])
+    loads[1].wait()
 
     pl.semaphore_wait(barrier, nrd - 1 + nfd - 1)
 
@@ -122,58 +133,57 @@
     def _():
         c_prev.start()
 
-    for i in range(3):
-        put_weight(wf, i, sw_ref[i].reshape(three, chans))
+    def put_cots(first, src):
+        for f in range(nf):
+            for h in range(strip):
+                rows = pl.ds(first + f * width, width)
+                high, low = split(src[f, h])
+                cots[0, h, rows, :] = high
+                cots[1, h, rows, :] = low
+
+    put_cots(0, cot_ref)
+    loads[2].wait()
     for k in range(3):
         put_weight(tb, k, tw_ref[k].T)
         put_weight(tf, k, tw_ref[k])
-    for f in range(nf):
-        for h in range(strip):
-            high, low = split(cot_ref[f, h])
-            cots[0, h, pl.ds(f * width, width), :] = high
-            cots[1, h, pl.ds(f * width, width), :] = low
-
-    def conv(src, row, weight, i):
-        return product(src[row, :, :three], src[row, :, three:], weight[i])
-
-    pre = [conv(xs, 1, wf, 1) + conv(xs, 2, wf, 2), conv(xs, 1, wf, 0) + conv(xs, 2, wf, 1)]
+    loads[3].wait()
+    for i in range(3):
+        put_weight(wf, i, sw_ref[i].reshape(three, chans))
+
+    def conv(src, row, count, weight, i):
+        rows = src[row : row + count].reshape(count * wide, 2 * three)
+        return product(rows[:, :three], rows[:, three:], weight[i])
+
+    middle = conv(xs, 1, 2, wf, 1)
+    pre = [middle[:wide] + conv(xs, 2, 1, wf, 2), middle[wide:] + conv(xs, 1, 1, wf, 0)]
     for i in range(3):
         put_weight(wb, i, jnp.concatenate([sw_ref[i, 2 - b].T for b in range(3)], axis=0))
 
+    def temporal(src, shift, weight, k):
+        rows = pl.ds(shift * width, wide)
+        both = [src[p, :, rows, :].reshape(strip * wide, chans) for p in range(2)]
+        return product(both[0], both[1], weight[k])
+
+    dact = temporal(cots, 0, tb, 0)
+    receive(c_prev, has_next, chalo)
+    put_cots(wide, chalo)
+    dact = dact + temporal(cots, 1, tb, 1) + temporal(cots, 2, tb, 2)
+
     receive(x_down, has_up, xhalo.at[0])
+    put_row(xs, 0, [xhalo[0, f] for f in range(nf)])
     receive(x_up, has_down, xhalo.at[1])
-    put_row(xs, 0, [xhalo[0, f] for f in range(nf)])
     put_row(xs, 3, [xhalo[1, f] for f in range(nf)])
-    pre = [pre[0] + conv(xs, 0, wf, 0), pre[1] + conv(xs, 3, wf, 2)]
-    receive(c_prev, has_next, chalo)
-    for f in range(nf):
-        for h in range(strip):
-            high, low = split(chalo[f, h])
-            cots[0, h, pl.ds(wide + f * width, width), :] = high
-            cots[1, h, pl.ds(wide + f * width, width), :] = low
+    pre = [pre[0] + conv(xs, 0, 1, wf, 0), pre[1] + conv(xs, 3, 1, wf, 2)]
 
     both_act, both_dpre = [], []
     for h in range(strip):
         sig = 1.0 / (1.0 + jnp.exp(-pre[h]))
         act_h = pre[h] * sig
         act[h] = act_h
-        dact = None
-        for k in range(3):
-            rows = pl.ds(k * width, wide)
-            term = product(cots[0, h, rows, :], cots[1, h, rows, :], tb[k])
-            dact = term if dact is None else dact + term
-        dpre_h = dact * sig * (1.0 + pre[h] * (1.0 - sig))
+        dpre_h = dact[h * wide : (h + 1) * wide] * sig * (1.0 + pre[h] * (1.0 - sig))
         dpre[h] = dpre_h
         both_act.append(act_h)
         both_dpre.append(dpre_h)
-
-    @pl.when(has_up)
-    def _():
-        d_up.start()
-
-    @pl.when(has_down)
-    def _():
-        d_down.start()
 
     @pl.when(has_next)
     def _():
@@ -195,7 +205,7 @@
         for j in range(3):
             terms[g, side, j] = term[:, j * chans : (j + 1) * chans]
 
-    spatial_terms(0, 0, 1)
+    spatial_terms(1, 0, 1)
     to_core = [None] * GROUPS
     to_rows = [None] * GROUPS
     to_z = [None] * GROUPS
@@ -248,53 +258,68 @@
 
     def finish(g):
         back[g].wait_recv()
-        gr_ref[g] = final[g]
-
-    def mixed():
-        receive(a_next, has_prev, ahalo)
+        stores.append(pltpu.make_async_copy(final.at[g], gr_hbm.at[g], store_sem.at[2 + g]))
+        stores[-1].start()
+
+    def put_acts(first, src):
         for h in range(strip):
-            for part, value in ((0, ahalo[h]), (1, act[h])):
-                high, low = split(value)
-                acts[0, h, pl.ds(part * wide, wide), :] = high
-                acts[1, h, pl.ds(part * wide, wide), :] = low
-        for h in range(strip):
-            total = None
-            for k in range(3):
-                rows = pl.ds((2 - k) * width, wide)
-                term = product(acts[0, h, rows, :], acts[1, h, rows, :], tf[k])
-                total = term if total is None else total + term
-            for f in range(nf):
-                mix_ref[f, h] = total[f * width : (f + 1) * width]
-
-    def image_gradient():
-        receive(d_down, has_up, dhalo.at[0])
-        receive(d_up, has_down, dhalo.at[1])
-        put_row(ds, 0, [dhalo[0, pl.ds(f * width, width)] for f in range(nf)])
-        put_row(ds, 3, [dhalo[1, pl.ds(f * width, width)] for f in range(nf)])
-        for h in range(strip):
-            put_row(ds, h + 1, [dpre[h, pl.ds(f * width, width)] for f in range(nf)])
-        for h in range(strip):
-            total = conv(ds, h + 2, wb, 0) + conv(ds, h + 1, wb, 1) + conv(ds, h, wb, 2)
-            for f in range(nf):
-                gi_ref[f, h] = total[f * width : (f + 1) * width]
+            high, low = split(src[h])
+            acts[0, h, pl.ds(first, wide), :] = high
+            acts[1, h, pl.ds(first, wide), :] = low
 
     start_core(0)
-    spatial_terms(1, 1, 0)
+    spatial_terms(0, 1, 0)
     spatial_terms(2, 1, 1)
     start_core(1)
     start_rows(0)
+    for h in range(strip):
+        put_row(ds, h + 1, [dpre[h, pl.ds(f * width, width)] for f in range(nf)])
     start_rows(1)
-    mixed()
+
+    @pl.when(has_up)
+    def _():
+        d_up.start()
+
+    @pl.when(has_down)
+    def _():
+        d_down.start()
+
+    put_acts(wide, act)
+    mixed = temporal(acts, 2, tf, 0)
+    receive(a_next, has_prev, ahalo)
+    put_acts(0, ahalo)
+    mixed = mixed + temporal(acts, 1, tf, 1) + temporal(acts, 0, tf, 2)
+    for h in range(strip):
+        for f in range(nf):
+            at = h * wide + f * width
+            mix_ref[f, h] = x_ref[f, h] + mixed[at : at + width]
+    stores.append(pltpu.make_async_copy(mix_ref, mix_hbm, store_sem.at[0]))
+    stores[-1].start()
     start_z(0)
-    image_gradient()
+
+    middle = conv(ds, 1, 2, wb, 1)
+    grad = [middle[:wide] + conv(ds, 2, 1, wb, 0), middle[wide:] + conv(ds, 1, 1, wb, 2)]
     start_z(1)
     start_around(0)
+    receive(d_down, has_up, dhalo.at[0])
+    put_row(ds, 0, [dhalo[0, pl.ds(f * width, width)] for f in range(nf)])
+    receive(d_up, has_down, dhalo.at[1])
+    put_row(ds, 3, [dhalo[1, pl.ds(f * width, width)] for f in range(nf)])
+    grad = [grad[0] + conv(ds, 0, 1, wb, 2), grad[1] + conv(ds, 3, 1, wb, 0)]
+    for h in range(strip):
+        for f in range(nf):
+            at = f * width
+            gi_ref[f, h] = cot_ref[f, h] + grad[h][at : at + width]
+    stores.append(pltpu.make_async_copy(gi_ref, gi_hbm, store_sem.at[1]))
+    stores[-1].start()
     start_around(1)
     start_back(0)
     start_back(1)
     finish(0)
     finish(1)
 
+    for copy in stores:
+        copy.wait()
     for copy in sent:
         copy.wait_send()
     for copy, there in (
@@ -302,6 +327,17 @@
         (a_next, has_next), (d_up, has_up), (d_down, has_down),
     ):
         pl.when(there)(copy.wait_send)
+
+
+def write(rows, mix_ref, gi_ref, gr_ref, out_ref, grad_ref, spatial_ref, temporal_ref, sem):
+    pairs = [(mix_ref, out_ref), (gi_ref, grad_ref), (gr_ref.at[0, 0, pl.ds(0, rows)], temporal_ref)]
+    for i, (g, side) in enumerate(((1, 0), (0, 1), (1, 1))):
+        pairs.append((gr_ref.at[g, side, pl.ds(0, rows)], spatial_ref.at[i]))
+    copies = [pltpu.make_async_copy(src, dst, sem.at[n]) for n, (src, dst) in enumerate(pairs)]
+    for copy in copies:
+        copy.start()
+    for copy in copies:
+        copy.wait()
 
 
 def per_device(nfd, nrd, images, spatial_weight, temporal_weight, cotangent):
@@ -312,17 +348,23 @@
     piece = -(-piece // 8) * 8
     factor = 1.0 / math.sqrt(nf * nfd * strip * nrd * width)
     n_sems = 6 + GROUPS * (2 + (nrd - 1) + 2 * (nz - 1))
-    vmem = pl.BlockSpec(memory_space=pltpu.VMEM)
-    mixed, gradient, grads = pl.pallas_call(
+    hbm = pl.BlockSpec(memory_space=pltpu.HBM)
+    operands = (images, spatial_weight, temporal_weight, cotangent)
+    results = pl.pallas_call(
         functools.partial(kernel, nfd, nrd, share, piece, factor),
         out_shape=(
             jax.ShapeDtypeStruct(images.shape, F32),
             jax.ShapeDtypeStruct(images.shape, F32),
             jax.ShapeDtypeStruct((GROUPS, 2, nz * piece, chans), F32),
         ),
-        in_specs=[vmem] * 4,
-        out_specs=(vmem,) * 3,
+        in_specs=[hbm] * 4,
+        out_specs=(hbm,) * 3,
         scratch_shapes=[
+            *(pltpu.VMEM(a.shape, F32) for a in operands),
+            pltpu.VMEM(images.shape, F32),
+            pltpu.VMEM(images.shape, F32),
+            pltpu.SemaphoreType.DMA((4,)),
+            pltpu.SemaphoreType.DMA((2 + GROUPS,)),
             pltpu.VMEM((strip + 2, wide, 2 * three), BF16),
             pltpu.VMEM((strip + 2, wide, 2 * three), BF16),
             pltpu.VMEM((3, three, 2 * chans), BF16),
@@ -349,12 +391,30 @@
             pltpu.SemaphoreType.DMA((n_sems,)),
         ],
         compiler_params=pltpu.CompilerParams(
-            collective_id=0, has_side_effects=True, vmem_limit_bytes=24 * 2**20
+            collective_id=0, has_side_effects=True, vmem_limit_bytes=VMEM_LIMIT
         ),
         cost_estimate=pl.CostEstimate(flops=1_400_000_000, bytes_accessed=2_000_000, transcendentals=50_000),
-    )(images, spatial_weight, temporal_weight, cotangent)
-    grads = grads[:, :, : 3 * share].reshape(GROUPS * 2, 3, share, chans).transpose(0, 1, 3, 2)
-    return images + mixed, cotangent + gradient, grads[1:], grads[0]
+    )(*operands)
+    out, gradient, spatial, temporal = pl.pallas_call(
+        functools.partial(write, 3 * share),
+        out_shape=(
+            jax.ShapeDtypeStruct(images.shape, F32),
+            jax.ShapeDtypeStruct(images.shape, F32),
+            jax.ShapeDtypeStruct((3, 3 * share, chans), F32),
+            jax.ShapeDtypeStruct((3 * share, chans), F32),
+        ),
+        in_specs=[hbm] * 3,
+        out_specs=(hbm,) * 4,
+        scratch_shapes=[pltpu.SemaphoreType.DMA((6,))],
+        compiler_params=pltpu.CompilerParams(vmem_limit_bytes=VMEM_LIMIT),
+        cost_estimate=pl.CostEstimate(flops=0, bytes_accessed=1_200_000, transcendentals=0),
+    )(*results)
+    return (
+        out,
+        gradient,
+        spatial.reshape(3, 3, share, chans).transpose(0, 1, 3, 2),
+        temporal.reshape(3, share, chans).transpose(0, 2, 1),
+    )
 
 
 def solution(mesh):

time: 38.4 us -> 50.3 us (1.31)
  the two profiles are of different devices: /device:TPU:3 before, /device:TPU:0 now
where the time goes in v2:
time: 50.3 us; the launch traced here: 49.6 us
  Pallas kernels  48.9 us (97%)
  between operations  0.64 us (1%)
    pallas_call x1, Pallas kernels, per_device(): pl.pallas_call(functools.partial(kernel, nfd, nrd, share, piece, factor),...  29.9 us
    pallas_call x1, Pallas kernels, per_device(): pl.pallas_call(functools.partial(write, 3 * share), out_shape=(jax.ShapeD...  19 us

profile of v2, /device:TPU:0, one launch (start us, length us, event | category | flops | bytes accessed | tf_op | source)
XLA Modules:
  0.0 49.6 jit_solution(13025411356465342734)
XLA Ops:
  0.6 29.9 %shard_map.75 = (f32[2,2,96,128]{3,2,1,0:T(8,128)}, f32[2,2,96,128]{3,2,1,0:T(8,128)}, f32[2,2,96,128]{3,2,1,0:T(8,128)}) custom-call(f32[2,2,96,128]{3,2,1,0:T(8,128)} %x_hbm.1, f32[3,3,128,128]{3,2,1,0:T(8,128)} %sw_hbm.1, f32[3,128,128]{2,1,0:T(8,128)} %tw_hbm.1, f32[2,2,96,128]{3,2,1,0:T(8,128)} %cot_hbm.1), custom_call_target="tpu_custom_call" | custom-call | flops 1400000000 | bytes 2000000 | tf_op jit(solution)/shard_map/pallas_call | solution.py:353
  30.5 19.0 %shard_map.76 = (f32[2,2,96,128]{3,2,1,0:T(8,128)}, f32[2,2,96,128]{3,2,1,0:T(8,128)}, f32[3,96,128]{2,1,0:T(8,128)}, f32[96,128]{1,0:T(8,128)}) custom-call(f32[2,2,96,128]{3,2,1,0:T(8,128)} %get-tuple-element.11.mix_ref, f32[2,2,96,128]{3,2,1,0:T(8,128)} %get-tuple-element.12.gi_ref, f32[2,2,96,128]{3,2,1,0:T(8,128)} %get-tuple-element.13.gr_ref), custom_call_target="tpu_custom_call" | custom-call | bytes 1200000 | tf_op jit(solution)/shard_map/pallas_call | solution.py:398

commit v3 on v2

--- a/solution.py
+++ b/solution.py
@@ -11,7 +11,7 @@
 MESH = pl.DeviceIdType.MESH
 F32, BF16 = jnp.float32, jnp.bfloat16
 GROUPS = 2
-VMEM_LIMIT = 60 * 2**20
+VMEM_LIMIT = 24 * 2**20
 
 
 def split(value):
@@ -51,8 +51,8 @@
 
 def kernel(
     nfd, nrd, share, piece, factor,
-    x_hbm, sw_hbm, tw_hbm, cot_hbm, mix_hbm, gi_hbm, gr_hbm,
-    x_ref, sw_ref, tw_ref, cot_ref, mix_ref, gi_ref, load_sem, store_sem, xs, ds, wf, wb, tf, tb, xhalo, chalo, ahalo, dhalo, act, dpre, cots, acts,
+    x_hbm, sw_hbm, tw_hbm, cot_hbm, mix_ref, gi_ref, gr_ref,
+    x_ref, sw_ref, tw_ref, cot_ref, load_sem, xs, ds, wf, wb, tf, tb, xhalo, chalo, ahalo, dhalo, act, dpre, cots, acts,
     terms, core_in, half, rows_in, plane, z_in, own, final, send_sem, recv_sem,
 ):
     nf, strip, width, chans = x_ref.shape
@@ -64,7 +64,7 @@
     nz = nfd // 2
     other = fr + 1 - 2 * core
     n_sems = [0]
-    sent, stores = [], []
+    sent = []
 
     def remote(src, dst, **where):
         n = n_sems[0]
@@ -258,8 +258,7 @@
 
     def finish(g):
         back[g].wait_recv()
-        stores.append(pltpu.make_async_copy(final.at[g], gr_hbm.at[g], store_sem.at[2 + g]))
-        stores[-1].start()
+        gr_ref[g] = final[g]
 
     def put_acts(first, src):
         for h in range(strip):
@@ -293,8 +292,6 @@
         for f in range(nf):
             at = h * wide + f * width
             mix_ref[f, h] = x_ref[f, h] + mixed[at : at + width]
-    stores.append(pltpu.make_async_copy(mix_ref, mix_hbm, store_sem.at[0]))
-    stores[-1].start()
     start_z(0)
 
     middle = conv(ds, 1, 2, wb, 1)
@@ -310,16 +307,12 @@
         for f in range(nf):
             at = f * width
             gi_ref[f, h] = cot_ref[f, h] + grad[h][at : at + width]
-    stores.append(pltpu.make_async_copy(gi_ref, gi_hbm, store_sem.at[1]))
-    stores[-1].start()
     start_around(1)
     start_back(0)
     start_back(1)
     finish(0)
     finish(1)
 
-    for copy in stores:
-        copy.wait()
     for copy in sent:
         copy.wait_send()
     for copy, there in (
@@ -348,23 +341,21 @@
     piece = -(-piece // 8) * 8
     factor = 1.0 / math.sqrt(nf * nfd * strip * nrd * width)
     n_sems = 6 + GROUPS * (2 + (nrd - 1) + 2 * (nz - 1))
-    hbm = pl.BlockSpec(memory_space=pltpu.HBM)
+    vmem, hbm = (pl.BlockSpec(memory_space=space) for space in (pltpu.VMEM, pltpu.HBM))
     operands = (images, spatial_weight, temporal_weight, cotangent)
+    operands = [pltpu.with_memory_space_constraint(a, pltpu.HBM) for a in operands]
     results = pl.pallas_call(
         functools.partial(kernel, nfd, nrd, share, piece, factor),
         out_shape=(
-            jax.ShapeDtypeStruct(images.shape, F32),
-            jax.ShapeDtypeStruct(images.shape, F32),
-            jax.ShapeDtypeStruct((GROUPS, 2, nz * piece, chans), F32),
+            pltpu.VMEM(images.shape, F32),
+            pltpu.VMEM(images.shape, F32),
+            pltpu.VMEM((GROUPS, 2, nz * piece, chans), F32),
         ),
         in_specs=[hbm] * 4,
-        out_specs=(hbm,) * 3,
+        out_specs=(vmem,) * 3,
         scratch_shapes=[
             *(pltpu.VMEM(a.shape, F32) for a in operands),
-            pltpu.VMEM(images.shape, F32),
-            pltpu.VMEM(images.shape, F32),
             pltpu.SemaphoreType.DMA((4,)),
-            pltpu.SemaphoreType.DMA((2 + GROUPS,)),
             pltpu.VMEM((strip + 2, wide, 2 * three), BF16),
             pltpu.VMEM((strip + 2, wide, 2 * three), BF16),
             pltpu.VMEM((3, three, 2 * chans), BF16),
@@ -403,7 +394,7 @@
             jax.ShapeDtypeStruct((3, 3 * share, chans), F32),
             jax.ShapeDtypeStruct((3 * share, chans), F32),
         ),
-        in_specs=[hbm] * 3,
+        in_specs=[vmem] * 3,
         out_specs=(hbm,) * 4,
         scratch_shapes=[pltpu.SemaphoreType.DMA((6,))],
         compiler_params=pltpu.CompilerParams(vmem_limit_bytes=VMEM_LIMIT),

time: 50.3 us -> 31.5 us (0.63); the launches traced: 49.6 us -> 31.3 us
  Pallas kernels: 48.9 us -> 30.7 us
    pallas_call x1, Pallas kernels: 19 us -> 0.85 us  [per_device(): pl.pallas_call(functools.partial(write, 3 * share), out_shape=(jax.ShapeD...]
where the time goes in v3:
time: 31.5 us; the launch traced here: 31.3 us
  Pallas kernels  30.7 us (97%)
  between operations  0.64 us (2%)
    pallas_call x1, Pallas kernels, per_device(): pl.pallas_call(functools.partial(kernel, nfd, nrd, share, piece, factor),...  29.9 us
    pallas_call x1, Pallas kernels, per_device(): pl.pallas_call(functools.partial(write, 3 * share), out_shape=(jax.ShapeD...  0.85 us

profile of v3, /device:TPU:0, one launch (start us, length us, event | category | flops | bytes accessed | tf_op | source)
XLA Modules:
  0.0 31.3 jit_solution(13190837394761297252)
XLA Ops:
  0.6 29.9 %shard_map.75 = (f32[2,2,96,128]{3,2,1,0:T(8,128)S(1)}, f32[2,2,96,128]{3,2,1,0:T(8,128)S(1)}, f32[2,2,96,128]{3,2,1,0:T(8,128)S(1)}) custom-call(f32[2,2,96,128]{3,2,1,0:T(8,128)} %x_hbm.1, f32[3,3,128,128]{3,2,1,0:T(8,128)} %sw_hbm.1, f32[3,128,128]{2,1,0:T(8,128)} %tw_hbm.1, f32[2,2,96,128]{3,2,1,0:T(8,128)} %cot_hbm.1), custom_call_target="tpu_custom_call" | custom-call | flops 1400000000 | bytes 2000000 | tf_op jit(solution)/shard_map/pallas_call | solution.py:347
  30.5 0.9 %shard_map.76 = (f32[2,2,96,128]{3,2,1,0:T(8,128)}, f32[2,2,96,128]{3,2,1,0:T(8,128)}, f32[3,96,128]{2,1,0:T(8,128)}, f32[96,128]{1,0:T(8,128)}) custom-call(f32[2,2,96,128]{3,2,1,0:T(8,128)S(1)} %get-tuple-element.11.mix_ref, f32[2,2,96,128]{3,2,1,0:T(8,128)S(1)} %get-tuple-element.12.gi_ref, f32[2,2,96,128]{3,2,1,0:T(8,128)S(1)} %get-tuple-element.13.gr_ref), custom_call_target="tpu_custom_call" | custom-call | bytes 1200000 | tf_op jit(solution)/shard_map/pallas_call | solution.py:389

commit v4 on v3

--- a/solution.py
+++ b/solution.py
@@ -10,7 +10,8 @@
 
 MESH = pl.DeviceIdType.MESH
 F32, BF16 = jnp.float32, jnp.bfloat16
-GROUPS = 2
+PER_CORE = 2
+GROUPS = 6 // PER_CORE
 VMEM_LIMIT = 24 * 2**20
 
 
@@ -94,20 +95,15 @@
     for o in range(1, nfd):
         pl.semaphore_signal(barrier, inc=1, device_id={"frames": lax.rem(fr + o, nfd)}, device_id_type=MESH)
 
-    loads[0].wait()
-    for h in range(strip):
-        put_row(xs, h + 1, [x_ref[f, h] for f in range(nf)])
-    loads[1].wait()
-
     pl.semaphore_wait(barrier, nrd - 1 + nfd - 1)
 
     has_up, has_down = ro > 0, ro < nrd - 1
     has_prev, has_next = fr > 0, fr < nfd - 1
     up, down = lax.rem(ro + nrd - 1, nrd), lax.rem(ro + 1, nrd)
     prev, following = lax.rem(fr + nfd - 1, nfd), lax.rem(fr + 1, nfd)
-    x_up = remote(x_ref.at[:, 0], xhalo.at[1], rows=up)
-    x_down = remote(x_ref.at[:, strip - 1], xhalo.at[0], rows=down)
-    c_prev = remote(cot_ref, chalo, frames=prev)
+    x_up = remote(x_hbm.at[:, 0], xhalo.at[1], rows=up)
+    x_down = remote(x_hbm.at[:, strip - 1], xhalo.at[0], rows=down)
+    c_prev = remote(cot_hbm, chalo, frames=prev)
     a_next = remote(act, ahalo, frames=following)
     d_up = remote(dpre.at[0], dhalo.at[1], rows=up)
     d_down = remote(dpre.at[strip - 1], dhalo.at[0], rows=down)
@@ -141,11 +137,14 @@
                 cots[0, h, rows, :] = high
                 cots[1, h, rows, :] = low
 
+    loads[0].wait()
+    for h in range(strip):
+        put_row(xs, h + 1, [x_ref[f, h] for f in range(nf)])
+    loads[1].wait()
     put_cots(0, cot_ref)
     loads[2].wait()
     for k in range(3):
         put_weight(tb, k, tw_ref[k].T)
-        put_weight(tf, k, tw_ref[k])
     loads[3].wait()
     for i in range(3):
         put_weight(wf, i, sw_ref[i].reshape(three, chans))
@@ -156,8 +155,6 @@
 
     middle = conv(xs, 1, 2, wf, 1)
     pre = [middle[:wide] + conv(xs, 2, 1, wf, 2), middle[wide:] + conv(xs, 1, 1, wf, 0)]
-    for i in range(3):
-        put_weight(wb, i, jnp.concatenate([sw_ref[i, 2 - b].T for b in range(3)], axis=0))
 
     def temporal(src, shift, weight, k):
         rows = pl.ds(shift * width, wide)
@@ -189,23 +186,27 @@
     def _():
         a_next.start()
 
+    def put_term(tap, value):
+        g, place = divmod(tap, 2 * PER_CORE)
+        terms[g, place // PER_CORE, place % PER_CORE] = value
+
     act_t = split(jnp.concatenate(both_act, axis=0).T)
     for k in range(3):
         rows = pl.ds(k * width, wide)
         c_high = cots[0, :, rows, :].reshape(strip * wide, chans)
         c_low = cots[1, :, rows, :].reshape(strip * wide, chans)
         term = dot(act_t[0], c_high) + dot(act_t[0], c_low) + dot(act_t[1], c_high)
-        terms[0, 0, k] = term.T
+        put_term(k, term.T)
     dpre_t = split(jnp.concatenate(both_dpre, axis=0).T)
 
-    def spatial_terms(i, g, side):
+    def spatial_terms(i, first):
         src = xs[i : i + strip].reshape(strip * wide, 2 * three)
         wide_term = dot(dpre_t[0], src)
         term = wide_term[:, :three] + wide_term[:, three:] + dot(dpre_t[1], src[:, :three])
         for j in range(3):
-            terms[g, side, j] = term[:, j * chans : (j + 1) * chans]
-
-    spatial_terms(1, 0, 1)
+            put_term(first + j, term[:, j * chans : (j + 1) * chans])
+
+    spatial_terms(1, 3)
     to_core = [None] * GROUPS
     to_rows = [None] * GROUPS
     to_z = [None] * GROUPS
@@ -229,9 +230,9 @@
         for o in range(1, nrd):
             to_rows[g][o - 1].wait_recv()
             total = total + rows_in[g, o - 1]
-        plane[g, : 3 * share] = total.reshape(3 * share, chans) * factor
-        if nz * piece > 3 * share:
-            plane[g, 3 * share :] = jnp.zeros((nz * piece - 3 * share, chans), F32)
+        plane[g, : PER_CORE * share] = total.reshape(PER_CORE * share, chans) * factor
+        if nz * piece > PER_CORE * share:
+            plane[g, PER_CORE * share :] = jnp.zeros((nz * piece - PER_CORE * share, chans), F32)
         to_z[g] = []
         for o in range(1, nz):
             target = lax.rem(z + o, nz)
@@ -267,13 +268,15 @@
             acts[1, h, pl.ds(first, wide), :] = low
 
     start_core(0)
-    spatial_terms(0, 1, 0)
-    spatial_terms(2, 1, 1)
+    spatial_terms(0, 6)
     start_core(1)
     start_rows(0)
+    spatial_terms(2, 9)
+    start_core(2)
+    start_rows(1)
     for h in range(strip):
         put_row(ds, h + 1, [dpre[h, pl.ds(f * width, width)] for f in range(nf)])
-    start_rows(1)
+    start_rows(2)
 
     @pl.when(has_up)
     def _():
@@ -283,35 +286,42 @@
     def _():
         d_down.start()
 
+    for k in range(3):
+        put_weight(tf, k, tw_ref[k])
     put_acts(wide, act)
     mixed = temporal(acts, 2, tf, 0)
     receive(a_next, has_prev, ahalo)
     put_acts(0, ahalo)
+    start_z(0)
     mixed = mixed + temporal(acts, 1, tf, 1) + temporal(acts, 0, tf, 2)
     for h in range(strip):
         for f in range(nf):
             at = h * wide + f * width
             mix_ref[f, h] = x_ref[f, h] + mixed[at : at + width]
-    start_z(0)
-
+    start_z(1)
+
+    for i in range(3):
+        put_weight(wb, i, jnp.concatenate([sw_ref[i, 2 - b].T for b in range(3)], axis=0))
+    start_around(0)
+    start_z(2)
     middle = conv(ds, 1, 2, wb, 1)
     grad = [middle[:wide] + conv(ds, 2, 1, wb, 0), middle[wide:] + conv(ds, 1, 1, wb, 2)]
-    start_z(1)
-    start_around(0)
+    start_around(1)
+    start_back(0)
     receive(d_down, has_up, dhalo.at[0])
     put_row(ds, 0, [dhalo[0, pl.ds(f * width, width)] for f in range(nf)])
     receive(d_up, has_down, dhalo.at[1])
     put_row(ds, 3, [dhalo[1, pl.ds(f * width, width)] for f in range(nf)])
+    start_around(2)
+    start_back(1)
     grad = [grad[0] + conv(ds, 0, 1, wb, 2), grad[1] + conv(ds, 3, 1, wb, 0)]
     for h in range(strip):
         for f in range(nf):
             at = f * width
             gi_ref[f, h] = cot_ref[f, h] + grad[h][at : at + width]
-    start_around(1)
-    start_back(0)
-    start_back(1)
-    finish(0)
-    finish(1)
+    start_back(2)
+    for g in range(GROUPS):
+        finish(g)
 
     for copy in sent:
         copy.wait_send()
@@ -322,10 +332,13 @@
         pl.when(there)(copy.wait_send)
 
 
-def write(rows, mix_ref, gi_ref, gr_ref, out_ref, grad_ref, spatial_ref, temporal_ref, sem):
-    pairs = [(mix_ref, out_ref), (gi_ref, grad_ref), (gr_ref.at[0, 0, pl.ds(0, rows)], temporal_ref)]
-    for i, (g, side) in enumerate(((1, 0), (0, 1), (1, 1))):
-        pairs.append((gr_ref.at[g, side, pl.ds(0, rows)], spatial_ref.at[i]))
+def write(share, mix_ref, gi_ref, gr_ref, out_ref, grad_ref, spatial_ref, temporal_ref, sem):
+    pairs = [(mix_ref, out_ref), (gi_ref, grad_ref)]
+    for tap in range(12):
+        g, place = divmod(tap, 2 * PER_CORE)
+        src = gr_ref.at[g, place // PER_CORE, pl.ds(place % PER_CORE * share, share)]
+        i = (1, 0, 2)[tap // 3 - 1]
+        pairs.append((src, temporal_ref.at[tap] if tap < 3 else spatial_ref.at[i, tap % 3]))
     copies = [pltpu.make_async_copy(src, dst, sem.at[n]) for n, (src, dst) in enumerate(pairs)]
     for copy in copies:
         copy.start()
@@ -337,7 +350,7 @@
     nf, strip, width, chans = images.shape
     wide, three = nf * width, 3 * chans
     nz, share = nfd // 2, chans // nrd
-    piece = -(-(3 * share) // nz)
+    piece = -(-(PER_CORE * share) // nz)
     piece = -(-piece // 8) * 8
     factor = 1.0 / math.sqrt(nf * nfd * strip * nrd * width)
     n_sems = 6 + GROUPS * (2 + (nrd - 1) + 2 * (nz - 1))
@@ -370,10 +383,10 @@
             pltpu.VMEM((strip, wide, chans), F32),
             pltpu.VMEM((2, strip, 2 * wide, chans), BF16),
             pltpu.VMEM((2, strip, 2 * wide, chans), BF16),
-            pltpu.VMEM((GROUPS, 2, 3, chans, chans), F32),
-            pltpu.VMEM((GROUPS, 3, chans, chans), F32),
-            pltpu.VMEM((GROUPS, 3, chans, chans), F32),
-            pltpu.VMEM((GROUPS, nrd - 1, 3, share, chans), F32),
+            pltpu.VMEM((GROUPS, 2, PER_CORE, chans, chans), F32),
+            pltpu.VMEM((GROUPS, PER_CORE, chans, chans), F32),
+            pltpu.VMEM((GROUPS, PER_CORE, chans, chans), F32),
+            pltpu.VMEM((GROUPS, nrd - 1, PER_CORE, share, chans), F32),
             pltpu.VMEM((GROUPS, nz * piece, chans), F32),
             pltpu.VMEM((GROUPS, nz - 1, piece, chans), F32),
             pltpu.VMEM((GROUPS, 1, piece, chans), F32),
@@ -387,24 +400,24 @@
         cost_estimate=pl.CostEstimate(flops=1_400_000_000, bytes_accessed=2_000_000, transcendentals=50_000),
     )(*operands)
     out, gradient, spatial, temporal = pl.pallas_call(
-        functools.partial(write, 3 * share),
+        functools.partial(write, share),
         out_shape=(
             jax.ShapeDtypeStruct(images.shape, F32),
             jax.ShapeDtypeStruct(images.shape, F32),
-            jax.ShapeDtypeStruct((3, 3 * share, chans), F32),
-            jax.ShapeDtypeStruct((3 * share, chans), F32),
+            jax.ShapeDtypeStruct((3, 3, share, chans), F32),
+            jax.ShapeDtypeStruct((3, share, chans), F32),
         ),
         in_specs=[vmem] * 3,
         out_specs=(hbm,) * 4,
-        scratch_shapes=[pltpu.SemaphoreType.DMA((6,))],
+        scratch_shapes=[pltpu.SemaphoreType.DMA((14,))],
         compiler_params=pltpu.CompilerParams(vmem_limit_bytes=VMEM_LIMIT),
         cost_estimate=pl.CostEstimate(flops=0, bytes_accessed=1_200_000, transcendentals=0),
     )(*results)
     return (
         out,
         gradient,
-        spatial.reshape(3, 3, share, chans).transpose(0, 1, 3, 2),
-        temporal.reshape(3, share, chans).transpose(0, 2, 1),
+        spatial.transpose(0, 1, 3, 2),
+        temporal.transpose(0, 2, 1),
     )
 
 

time: 31.5 us -> 31.7 us (level)
  no operation moved by 1% of the time
where the time goes in v4:
time: 31.7 us; the launch traced here: 31.5 us
  Pallas kernels  30.9 us (97%)
  between operations  0.64 us (2%)
    pallas_call x1, Pallas kernels, per_device(): pl.pallas_call(functools.partial(kernel, nfd, nrd, share, piece, factor),...  30 us
    pallas_call x1, Pallas kernels, per_device(): pl.pallas_call(functools.partial(write, share), out_shape=(jax.ShapeDtype...  0.92 us

profile of v4, /device:TPU:0, one launch (start us, length us, event | category | flops | bytes accessed | tf_op | source)
XLA Modules:
  0.0 31.5 jit_solution(4741503994318369130)
XLA Ops:
  0.6 30.0 %shard_map.75 = (f32[2,2,96,128]{3,2,1,0:T(8,128)S(1)}, f32[2,2,96,128]{3,2,1,0:T(8,128)S(1)}, f32[3,2,64,128]{3,2,1,0:T(8,128)S(1)}) custom-call(f32[2,2,96,128]{3,2,1,0:T(8,128)} %x_hbm.1, f32[3,3,128,128]{3,2,1,0:T(8,128)} %sw_hbm.1, f32[3,128,128]{2,1,0:T(8,128)} %tw_hbm.1, f32[2,2,96,128]{3,2,1,0:T(8,128)} %cot_hbm.1), custom_call_target="tpu_custom_call" | custom-call | flops 1400000000 | bytes 2000000 | tf_op jit(solution)/shard_map/pallas_call | solution.py:360
  30.6 0.9 %shard_map.76 = (f32[2,2,96,128]{3,2,1,0:T(8,128)}, f32[2,2,96,128]{3,2,1,0:T(8,128)}, f32[3,3,32,128]{3,2,1,0:T(8,128)}, f32[3,32,128]{2,1,0:T(8,128)}) custom-call(f32[2,2,96,128]{3,2,1,0:T(8,128)S(1)} %get-tuple-element.11.mix_ref, f32[2,2,96,128]{3,2,1,0:T(8,128)S(1)} %get-tuple-element.12.gi_ref, f32[3,2,64,128]{3,2,1,0:T(8,128)S(1)} %get-tuple-element.13.gr_ref), custom_call_target="tpu_custom_call" | custom-call | bytes 1200000 | tf_op jit(solution)/shard_map/pallas_call | solution.py:402

commit v5 on v4

--- a/solution.py
+++ b/solution.py
@@ -31,10 +31,10 @@
     dst[index, :, n:] = low
 
 
-def product(high, low, both):
-    n = both.shape[1] // 2
-    wide = dot(high, both)
-    return wide[:, :n] + wide[:, n:] + dot(low, both[:, :n])
+def product(stacked, both):
+    m, n = stacked.shape[0] // 2, both.shape[1] // 2
+    wide = dot(stacked, both)
+    return wide[:m, :n] + (wide[:m, n:] + wide[m:, :n] + wide[m:, n:])
 
 
 def put_row(dst, row, frames):
@@ -46,8 +46,8 @@
         rows = pl.ds(f * width, width)
         for b, moved in enumerate((before, value, after)):
             high, low = split(moved)
-            dst[row, rows, b * chans : (b + 1) * chans] = high
-            dst[row, rows, (3 + b) * chans : (4 + b) * chans] = low
+            dst[0, row, rows, b * chans : (b + 1) * chans] = high
+            dst[1, row, rows, b * chans : (b + 1) * chans] = low
 
 
 def kernel(
@@ -150,16 +150,14 @@
         put_weight(wf, i, sw_ref[i].reshape(three, chans))
 
     def conv(src, row, count, weight, i):
-        rows = src[row : row + count].reshape(count * wide, 2 * three)
-        return product(rows[:, :three], rows[:, three:], weight[i])
+        return product(src[:, row : row + count].reshape(2 * count * wide, three), weight[i])
 
     middle = conv(xs, 1, 2, wf, 1)
     pre = [middle[:wide] + conv(xs, 2, 1, wf, 2), middle[wide:] + conv(xs, 1, 1, wf, 0)]
 
     def temporal(src, shift, weight, k):
         rows = pl.ds(shift * width, wide)
-        both = [src[p, :, rows, :].reshape(strip * wide, chans) for p in range(2)]
-        return product(both[0], both[1], weight[k])
+        return product(src[:, :, rows, :].reshape(2 * strip * wide, chans), weight[k])
 
     dact = temporal(cots, 0, tb, 0)
     receive(c_prev, has_next, chalo)
@@ -186,23 +184,23 @@
     def _():
         a_next.start()
 
+    def stack(strips):
+        return jnp.concatenate(split(jnp.concatenate(strips, axis=0).T), axis=0)
+
     def put_term(tap, value):
         g, place = divmod(tap, 2 * PER_CORE)
         terms[g, place // PER_CORE, place % PER_CORE] = value
 
-    act_t = split(jnp.concatenate(both_act, axis=0).T)
+    act_t = stack(both_act)
     for k in range(3):
         rows = pl.ds(k * width, wide)
-        c_high = cots[0, :, rows, :].reshape(strip * wide, chans)
-        c_low = cots[1, :, rows, :].reshape(strip * wide, chans)
-        term = dot(act_t[0], c_high) + dot(act_t[0], c_low) + dot(act_t[1], c_high)
-        put_term(k, term.T)
-    dpre_t = split(jnp.concatenate(both_dpre, axis=0).T)
+        both = [cots[p, :, rows, :].reshape(strip * wide, chans) for p in range(2)]
+        put_term(k, product(act_t, jnp.concatenate(both, axis=1)).T)
+    dpre_t = stack(both_dpre)
 
     def spatial_terms(i, first):
-        src = xs[i : i + strip].reshape(strip * wide, 2 * three)
-        wide_term = dot(dpre_t[0], src)
-        term = wide_term[:, :three] + wide_term[:, three:] + dot(dpre_t[1], src[:, :three])
+        both = [xs[p, i : i + strip].reshape(strip * wide, three) for p in range(2)]
+        term = product(dpre_t, jnp.concatenate(both, axis=1))
         for j in range(3):
             put_term(first + j, term[:, j * chans : (j + 1) * chans])
 
@@ -369,8 +367,8 @@
         scratch_shapes=[
             *(pltpu.VMEM(a.shape, F32) for a in operands),
             pltpu.SemaphoreType.DMA((4,)),
-            pltpu.VMEM((strip + 2, wide, 2 * three), BF16),
-            pltpu.VMEM((strip + 2, wide, 2 * three), BF16),
+            pltpu.VMEM((2, strip + 2, wide, three), BF16),
+            pltpu.VMEM((2, strip + 2, wide, three), BF16),
             pltpu.VMEM((3, three, 2 * chans), BF16),
             pltpu.VMEM((3, three, 2 * chans), BF16),
             pltpu.VMEM((3, chans, 2 * chans), BF16),

time: 31.7 us -> 32.1 us (1.013)
  Pallas kernels: 30.9 us -> 31.3 us
    pallas_call x1, Pallas kernels: 30 us -> 30.3 us  [per_device(): pl.pallas_call(functools.partial(kernel, nfd, nrd, share, piece, factor),...]
where the time goes in v5:
time: 32.1 us; the launch traced here: 31.9 us
  Pallas kernels  31.3 us (98%)
  between operations  0.64 us (2%)
    pallas_call x1, Pallas kernels, per_device(): pl.pallas_call(functools.partial(kernel, nfd, nrd, share, piece, factor),...  30.3 us
    pallas_call x1, Pallas kernels, per_device(): pl.pallas_call(functools.partial(write, share), out_shape=(jax.ShapeDtype...  0.92 us

profile of v5, /device:TPU:0, one launch (start us, length us, event | category | flops | bytes accessed | tf_op | source)
XLA Modules:
  0.0 31.9 jit_solution(3197493711450517362)
XLA Ops:
  0.6 30.3 %shard_map.75 = (f32[2,2,96,128]{3,2,1,0:T(8,128)S(1)}, f32[2,2,96,128]{3,2,1,0:T(8,128)S(1)}, f32[3,2,64,128]{3,2,1,0:T(8,128)S(1)}) custom-call(f32[2,2,96,128]{3,2,1,0:T(8,128)} %x_hbm.1, f32[3,3,128,128]{3,2,1,0:T(8,128)} %sw_hbm.1, f32[3,128,128]{2,1,0:T(8,128)} %tw_hbm.1, f32[2,2,96,128]{3,2,1,0:T(8,128)} %cot_hbm.1), custom_call_target="tpu_custom_call" | custom-call | flops 1400000000 | bytes 2000000 | tf_op jit(solution)/shard_map/pallas_call | solution.py:358
  31.0 0.9 %shard_map.76 = (f32[2,2,96,128]{3,2,1,0:T(8,128)}, f32[2,2,96,128]{3,2,1,0:T(8,128)}, f32[3,3,32,128]{3,2,1,0:T(8,128)}, f32[3,32,128]{2,1,0:T(8,128)}) custom-call(f32[2,2,96,128]{3,2,1,0:T(8,128)S(1)} %get-tuple-element.11.mix_ref, f32[2,2,96,128]{3,2,1,0:T(8,128)S(1)} %get-tuple-element.12.gi_ref, f32[3,2,64,128]{3,2,1,0:T(8,128)S(1)} %get-tuple-element.13.gr_ref), custom_call_target="tpu_custom_call" | custom-call | bytes 1200000 | tf_op jit(solution)/shard_map/pallas_call | solution.py:400

commit v6 on v5

--- a/solution.py
+++ b/solution.py
@@ -272,8 +272,6 @@
     spatial_terms(2, 9)
     start_core(2)
     start_rows(1)
-    for h in range(strip):
-        put_row(ds, h + 1, [dpre[h, pl.ds(f * width, width)] for f in range(nf)])
     start_rows(2)
 
     @pl.when(has_up)
@@ -287,37 +285,38 @@
     for k in range(3):
         put_weight(tf, k, tw_ref[k])
     put_acts(wide, act)
+    start_z(0)
     mixed = temporal(acts, 2, tf, 0)
     receive(a_next, has_prev, ahalo)
     put_acts(0, ahalo)
-    start_z(0)
     mixed = mixed + temporal(acts, 1, tf, 1) + temporal(acts, 0, tf, 2)
     for h in range(strip):
         for f in range(nf):
             at = h * wide + f * width
             mix_ref[f, h] = x_ref[f, h] + mixed[at : at + width]
     start_z(1)
-
+    for h in range(strip):
+        put_row(ds, h + 1, [dpre[h, pl.ds(f * width, width)] for f in range(nf)])
+    start_around(0)
     for i in range(3):
         put_weight(wb, i, jnp.concatenate([sw_ref[i, 2 - b].T for b in range(3)], axis=0))
-    start_around(0)
     start_z(2)
+    start_around(1)
     middle = conv(ds, 1, 2, wb, 1)
     grad = [middle[:wide] + conv(ds, 2, 1, wb, 0), middle[wide:] + conv(ds, 1, 1, wb, 2)]
-    start_around(1)
     start_back(0)
+    start_around(2)
+    start_back(1)
+    start_back(2)
     receive(d_down, has_up, dhalo.at[0])
     put_row(ds, 0, [dhalo[0, pl.ds(f * width, width)] for f in range(nf)])
     receive(d_up, has_down, dhalo.at[1])
     put_row(ds, 3, [dhalo[1, pl.ds(f * width, width)] for f in range(nf)])
-    start_around(2)
-    start_back(1)
     grad = [grad[0] + conv(ds, 0, 1, wb, 2), grad[1] + conv(ds, 3, 1, wb, 0)]
     for h in range(strip):
         for f in range(nf):
             at = f * width
             gi_ref[f, h] = cot_ref[f, h] + grad[h][at : at + width]
-    start_back(2)
     for g in range(GROUPS):
         finish(g)
 

time: 32.1 us -> 32.1 us (level)
  no operation moved by 1% of the time
where the time goes in v6:
time: 32.1 us; the launch traced here: 31.9 us
  Pallas kernels  31.3 us (98%)
  between operations  0.64 us (2%)
    pallas_call x1, Pallas kernels, per_device(): pl.pallas_call(functools.partial(kernel, nfd, nrd, share, piece, factor),...  30.3 us
    pallas_call x1, Pallas kernels, per_device(): pl.pallas_call(functools.partial(write, share), out_shape=(jax.ShapeDtype...  0.92 us

profile of v6, /device:TPU:0, one launch (start us, length us, event | category | flops | bytes accessed | tf_op | source)
XLA Modules:
  0.0 31.9 jit_solution(16953836509930515187)
XLA Ops:
  0.6 30.3 %shard_map.75 = (f32[2,2,96,128]{3,2,1,0:T(8,128)S(1)}, f32[2,2,96,128]{3,2,1,0:T(8,128)S(1)}, f32[3,2,64,128]{3,2,1,0:T(8,128)S(1)}) custom-call(f32[2,2,96,128]{3,2,1,0:T(8,128)} %x_hbm.1, f32[3,3,128,128]{3,2,1,0:T(8,128)} %sw_hbm.1, f32[3,128,128]{2,1,0:T(8,128)} %tw_hbm.1, f32[2,2,96,128]{3,2,1,0:T(8,128)} %cot_hbm.1), custom_call_target="tpu_custom_call" | custom-call | flops 1400000000 | bytes 2000000 | tf_op jit(solution)/shard_map/pallas_call | solution.py:357
  31.0 0.9 %shard_map.76 = (f32[2,2,96,128]{3,2,1,0:T(8,128)}, f32[2,2,96,128]{3,2,1,0:T(8,128)}, f32[3,3,32,128]{3,2,1,0:T(8,128)}, f32[3,32,128]{2,1,0:T(8,128)}) custom-call(f32[2,2,96,128]{3,2,1,0:T(8,128)S(1)} %get-tuple-element.11.mix_ref, f32[2,2,96,128]{3,2,1,0:T(8,128)S(1)} %get-tuple-element.12.gi_ref, f32[3,2,64,128]{3,2,1,0:T(8,128)S(1)} %get-tuple-element.13.gr_ref), custom_call_target="tpu_custom_call" | custom-call | bytes 1200000 | tf_op jit(solution)/shard_map/pallas_call | solution.py:399

commit v7 on v6

--- a/solution.py
+++ b/solution.py
@@ -10,7 +10,7 @@
 
 MESH = pl.DeviceIdType.MESH
 F32, BF16 = jnp.float32, jnp.bfloat16
-PER_CORE = 2
+PER_CORE = 3
 GROUPS = 6 // PER_CORE
 VMEM_LIMIT = 24 * 2**20
 
@@ -89,6 +89,8 @@
     ]
     for load in loads:
         load.start()
+    for halo in (xhalo, chalo, ahalo, dhalo):
+        halo[...] = jnp.zeros(halo.shape, F32)
     barrier = pltpu.get_barrier_semaphore()
     for o in range(1, nrd):
         pl.semaphore_signal(barrier, inc=1, device_id={"rows": lax.rem(ro + o, nrd)}, device_id_type=MESH)
@@ -108,14 +110,10 @@
     d_up = remote(dpre.at[0], dhalo.at[1], rows=up)
     d_down = remote(dpre.at[strip - 1], dhalo.at[0], rows=down)
 
-    def receive(copy, there, zeroed):
+    def receive(copy, there):
         @pl.when(there)
         def _():
             copy.wait_recv()
-
-        @pl.when(jnp.logical_not(there))
-        def _():
-            zeroed[...] = jnp.zeros(zeroed.shape, F32)
 
     @pl.when(has_up)
     def _():
@@ -160,13 +158,13 @@
         return product(src[:, :, rows, :].reshape(2 * strip * wide, chans), weight[k])
 
     dact = temporal(cots, 0, tb, 0)
-    receive(c_prev, has_next, chalo)
+    receive(c_prev, has_next)
     put_cots(wide, chalo)
     dact = dact + temporal(cots, 1, tb, 1) + temporal(cots, 2, tb, 2)
 
-    receive(x_down, has_up, xhalo.at[0])
+    receive(x_down, has_up)
     put_row(xs, 0, [xhalo[0, f] for f in range(nf)])
-    receive(x_up, has_down, xhalo.at[1])
+    receive(x_up, has_down)
     put_row(xs, 3, [xhalo[1, f] for f in range(nf)])
     pre = [pre[0] + conv(xs, 0, 1, wf, 0), pre[1] + conv(xs, 3, 1, wf, 2)]
 
@@ -225,8 +223,9 @@
 
     def start_z(g):
         total = half[g, :, pl.ds(pl.multiple_of(ro * share, 8), share), :]
+        for copy in to_rows[g]:
+            copy.wait_recv()
         for o in range(1, nrd):
-            to_rows[g][o - 1].wait_recv()
             total = total + rows_in[g, o - 1]
         plane[g, : PER_CORE * share] = total.reshape(PER_CORE * share, chans) * factor
         if nz * piece > PER_CORE * share:
@@ -240,8 +239,9 @@
     def start_around(g):
         mine = pl.ds(pl.multiple_of(z * piece, 8), piece)
         total = plane[g, mine]
+        for copy in to_z[g]:
+            copy.wait_recv()
         for o in range(1, nz):
-            to_z[g][o - 1].wait_recv()
             total = total + z_in[g, o - 1]
         own[g, 0] = total
         final[g, core, mine] = total
@@ -267,12 +267,10 @@
 
     start_core(0)
     spatial_terms(0, 6)
+    spatial_terms(2, 9)
     start_core(1)
     start_rows(0)
-    spatial_terms(2, 9)
-    start_core(2)
     start_rows(1)
-    start_rows(2)
 
     @pl.when(has_up)
     def _():
@@ -285,32 +283,29 @@
     for k in range(3):
         put_weight(tf, k, tw_ref[k])
     put_acts(wide, act)
-    start_z(0)
     mixed = temporal(acts, 2, tf, 0)
-    receive(a_next, has_prev, ahalo)
+    receive(a_next, has_prev)
     put_acts(0, ahalo)
     mixed = mixed + temporal(acts, 1, tf, 1) + temporal(acts, 0, tf, 2)
     for h in range(strip):
         for f in range(nf):
             at = h * wide + f * width
             mix_ref[f, h] = x_ref[f, h] + mixed[at : at + width]
-    start_z(1)
+    start_z(0)
     for h in range(strip):
         put_row(ds, h + 1, [dpre[h, pl.ds(f * width, width)] for f in range(nf)])
+    start_z(1)
     start_around(0)
     for i in range(3):
         put_weight(wb, i, jnp.concatenate([sw_ref[i, 2 - b].T for b in range(3)], axis=0))
-    start_z(2)
     start_around(1)
+    start_back(0)
     middle = conv(ds, 1, 2, wb, 1)
     grad = [middle[:wide] + conv(ds, 2, 1, wb, 0), middle[wide:] + conv(ds, 1, 1, wb, 2)]
-    start_back(0)
-    start_around(2)
     start_back(1)
-    start_back(2)
-    receive(d_down, has_up, dhalo.at[0])
+    receive(d_down, has_up)
     put_row(ds, 0, [dhalo[0, pl.ds(f * width, width)] for f in range(nf)])
-    receive(d_up, has_down, dhalo.at[1])
+    receive(d_up, has_down)
     put_row(ds, 3, [dhalo[1, pl.ds(f * width, width)] for f in range(nf)])
     grad = [grad[0] + conv(ds, 0, 1, wb, 2), grad[1] + conv(ds, 3, 1, wb, 0)]
     for h in range(strip):

time: 32.1 us -> 32 us (level)
  no operation moved by 1% of the time
where the time goes in v7:
time: 32 us; the launch traced here: 31.8 us
  Pallas kernels  31.2 us (98%)
  between operations  0.64 us (2%)
    pallas_call x1, Pallas kernels, per_device(): pl.pallas_call(functools.partial(kernel, nfd, nrd, share, piece, factor),...  30.3 us
    pallas_call x1, Pallas kernels, per_device(): pl.pallas_call(functools.partial(write, share), out_shape=(jax.ShapeDtype...  0.92 us

profile of v7, /device:TPU:0, one launch (start us, length us, event | category | flops | bytes accessed | tf_op | source)
XLA Modules:
  0.0 31.8 jit_solution(2669734544503707595)
XLA Ops:
  0.6 30.3 %shard_map.75 = (f32[2,2,96,128]{3,2,1,0:T(8,128)S(1)}, f32[2,2,96,128]{3,2,1,0:T(8,128)S(1)}, f32[2,2,96,128]{3,2,1,0:T(8,128)S(1)}) custom-call(f32[2,2,96,128]{3,2,1,0:T(8,128)} %x_hbm.1, f32[3,3,128,128]{3,2,1,0:T(8,128)} %sw_hbm.1, f32[3,128,128]{2,1,0:T(8,128)} %tw_hbm.1, f32[2,2,96,128]{3,2,1,0:T(8,128)} %cot_hbm.1), custom_call_target="tpu_custom_call" | custom-call | flops 1400000000 | bytes 2000000 | tf_op jit(solution)/shard_map/pallas_call | solution.py:352
  30.9 0.9 %shard_map.76 = (f32[2,2,96,128]{3,2,1,0:T(8,128)}, f32[2,2,96,128]{3,2,1,0:T(8,128)}, f32[3,3,32,128]{3,2,1,0:T(8,128)}, f32[3,32,128]{2,1,0:T(8,128)}) custom-call(f32[2,2,96,128]{3,2,1,0:T(8,128)S(1)} %get-tuple-element.11.mix_ref, f32[2,2,96,128]{3,2,1,0:T(8,128)S(1)} %get-tuple-element.12.gi_ref, f32[2,2,96,128]{3,2,1,0:T(8,128)S(1)} %get-tuple-element.13.gr_ref), custom_call_target="tpu_custom_call" | custom-call | bytes 1200000 | tf_op jit(solution)/shard_map/pallas_call | solution.py:394

commit v8 on v7

--- a/solution.py
+++ b/solution.py
@@ -54,7 +54,7 @@
     nfd, nrd, share, piece, factor,
     x_hbm, sw_hbm, tw_hbm, cot_hbm, mix_ref, gi_ref, gr_ref,
     x_ref, sw_ref, tw_ref, cot_ref, load_sem, xs, ds, wf, wb, tf, tb, xhalo, chalo, ahalo, dhalo, act, dpre, cots, acts,
-    terms, core_in, half, rows_in, plane, z_in, own, final, send_sem, recv_sem,
+    terms, core_in, half, rows_in, passed, plane, z_in, own, final, send_sem, recv_sem,
 ):
     nf, strip, width, chans = x_ref.shape
     assert nf == 2 and strip == 2
@@ -203,6 +203,15 @@
             put_term(first + j, term[:, j * chans : (j + 1) * chans])
 
     spatial_terms(1, 3)
+    two_steps = nrd == 4
+    along = ro + 1 - 2 * lax.rem(ro, 2)
+    across = ro + 2 - 4 * lax.div(ro, 2)
+    first = along * (1 - core) + across * core
+    second = across * (1 - core) + along * core
+
+    def rows_of(target):
+        return pl.ds(pl.multiple_of(target * share, 8), share)
+
     to_core = [None] * GROUPS
     to_rows = [None] * GROUPS
     to_z = [None] * GROUPS
@@ -215,18 +224,29 @@
     def start_rows(g):
         to_core[g].wait_recv()
         half[g] = terms[g, core] + core_in[g]
+        if two_steps:
+            to_rows[g] = [
+                send(half.at[g, :, rows_of(nrd - 1 - ro), :], rows_in.at[g, 1], rows=first),
+                send(half.at[g, :, rows_of(first), :], rows_in.at[g, 0], rows=first),
+            ]
+            return
         to_rows[g] = []
         for o in range(1, nrd):
             target = lax.rem(ro + o, nrd)
-            part = pl.ds(pl.multiple_of(target * share, 8), share)
-            to_rows[g].append(send(half.at[g, :, part, :], rows_in.at[g, o - 1], rows=target))
+            to_rows[g].append(send(half.at[g, :, rows_of(target), :], rows_in.at[g, o - 1], rows=target))
+
+    def forward_rows(g):
+        if two_steps:
+            to_rows[g].pop(0).wait_recv()
+            passed[g] = half[g, :, rows_of(second), :] + rows_in[g, 1]
+            to_rows[g].append(send(passed.at[g], rows_in.at[g, 2], rows=second))
 
     def start_z(g):
-        total = half[g, :, pl.ds(pl.multiple_of(ro * share, 8), share), :]
+        total = half[g, :, rows_of(ro), :]
         for copy in to_rows[g]:
             copy.wait_recv()
-        for o in range(1, nrd):
-            total = total + rows_in[g, o - 1]
+        for o in (0, 2) if two_steps else range(nrd - 1):
+            total = total + rows_in[g, o]
         plane[g, : PER_CORE * share] = total.reshape(PER_CORE * share, chans) * factor
         if nz * piece > PER_CORE * share:
             plane[g, PER_CORE * share :] = jnp.zeros((nz * piece - PER_CORE * share, chans), F32)
@@ -272,18 +292,21 @@
     start_rows(0)
     start_rows(1)
 
-    @pl.when(has_up)
-    def _():
-        d_up.start()
-
-    @pl.when(has_down)
-    def _():
-        d_down.start()
-
     for k in range(3):
         put_weight(tf, k, tw_ref[k])
     put_acts(wide, act)
+    forward_rows(0)
     mixed = temporal(acts, 2, tf, 0)
+    forward_rows(1)
+
+    @pl.when(has_up)
+    def _():
+        d_up.start()
+
+    @pl.when(has_down)
+    def _():
+        d_down.start()
+
     receive(a_next, has_prev)
     put_acts(0, ahalo)
     mixed = mixed + temporal(acts, 1, tf, 1) + temporal(acts, 0, tf, 2)
@@ -379,6 +402,7 @@
             pltpu.VMEM((GROUPS, PER_CORE, chans, chans), F32),
             pltpu.VMEM((GROUPS, PER_CORE, chans, chans), F32),
             pltpu.VMEM((GROUPS, nrd - 1, PER_CORE, share, chans), F32),
+            pltpu.VMEM((GROUPS, PER_CORE, share, chans), F32),
             pltpu.VMEM((GROUPS, nz * piece, chans), F32),
             pltpu.VMEM((GROUPS, nz - 1, piece, chans), F32),
             pltpu.VMEM((GROUPS, 1, piece, chans), F32),

time: 32 us -> 32.3 us (level)
  no operation moved by 1% of the time
where the time goes in v8:
time: 32.3 us; the launch traced here: 32 us
  Pallas kernels  31.4 us (97%)
  between operations  0.64 us (2%)
    pallas_call x1, Pallas kernels, per_device(): pl.pallas_call(functools.partial(kernel, nfd, nrd, share, piece, factor),...  30.4 us
    pallas_call x1, Pallas kernels, per_device(): pl.pallas_call(functools.partial(write, share), out_shape=(jax.ShapeDtype...  0.92 us

profile of v8, /device:TPU:0, one launch (start us, length us, event | category | flops | bytes accessed | tf_op | source)
XLA Modules:
  0.0 32.0 jit_solution(4096629763865649118)
XLA Ops:
  0.6 30.4 %shard_map.75 = (f32[2,2,96,128]{3,2,1,0:T(8,128)S(1)}, f32[2,2,96,128]{3,2,1,0:T(8,128)S(1)}, f32[2,2,96,128]{3,2,1,0:T(8,128)S(1)}) custom-call(f32[2,2,96,128]{3,2,1,0:T(8,128)} %x_hbm.1, f32[3,3,128,128]{3,2,1,0:T(8,128)} %sw_hbm.1, f32[3,128,128]{2,1,0:T(8,128)} %tw_hbm.1, f32[2,2,96,128]{3,2,1,0:T(8,128)} %cot_hbm.1), custom_call_target="tpu_custom_call" | custom-call | flops 1400000000 | bytes 2000000 | tf_op jit(solution)/shard_map/pallas_call | solution.py:375
  31.1 0.9 %shard_map.76 = (f32[2,2,96,128]{3,2,1,0:T(8,128)}, f32[2,2,96,128]{3,2,1,0:T(8,128)}, f32[3,3,32,128]{3,2,1,0:T(8,128)}, f32[3,32,128]{2,1,0:T(8,128)}) custom-call(f32[2,2,96,128]{3,2,1,0:T(8,128)S(1)} %get-tuple-element.11.mix_ref, f32[2,2,96,128]{3,2,1,0:T(8,128)S(1)} %get-tuple-element.12.gi_ref, f32[2,2,96,128]{3,2,1,0:T(8,128)S(1)} %get-tuple-element.13.gr_ref), custom_call_target="tpu_custom_call" | custom-call | bytes 1200000 | tf_op jit(solution)/shard_map/pallas_call | solution.py:418

commit v9 on v7

--- a/solution.py
+++ b/solution.py
@@ -37,23 +37,30 @@
     return wide[:m, :n] + (wide[:m, n:] + wide[m:, :n] + wide[m:, n:])
 
 
-def put_row(dst, row, frames):
-    width, chans = frames[0].shape
+def put_row(dst, row, f, value):
+    width, chans = value.shape
     at = lax.broadcasted_iota(jnp.int32, (width, chans), 0)
-    for f, value in enumerate(frames):
-        before = jnp.where(at == 0, 0.0, pltpu.roll(value, 1, 0))
-        after = jnp.where(at == width - 1, 0.0, pltpu.roll(value, width - 1, 0))
-        rows = pl.ds(f * width, width)
-        for b, moved in enumerate((before, value, after)):
-            high, low = split(moved)
-            dst[0, row, rows, b * chans : (b + 1) * chans] = high
-            dst[1, row, rows, b * chans : (b + 1) * chans] = low
+    before = jnp.where(at == 0, 0.0, pltpu.roll(value, 1, 0))
+    after = jnp.where(at == width - 1, 0.0, pltpu.roll(value, width - 1, 0))
+    rows = frame_rows(f, width)
+    for b, moved in enumerate((before, value, after)):
+        high, low = split(moved)
+        dst[0, row, rows, b * chans : (b + 1) * chans] = high
+        dst[1, row, rows, b * chans : (b + 1) * chans] = low
+
+
+def frame_rows(f, width, count=1):
+    return pl.ds(pl.multiple_of(f * width, 32), count * width)
+
+
+def each(count, body):
+    lax.fori_loop(0, count, lambda n, _: (body(n), 0)[1], 0)
 
 
 def kernel(
     nfd, nrd, share, piece, factor,
     x_hbm, sw_hbm, tw_hbm, cot_hbm, mix_ref, gi_ref, gr_ref,
-    x_ref, sw_ref, tw_ref, cot_ref, load_sem, xs, ds, wf, wb, tf, tb, xhalo, chalo, ahalo, dhalo, act, dpre, cots, acts,
+    x_ref, sw_ref, tw_ref, cot_ref, load_sem, pre, dact, act_t, dpre_t, xs, ds, wf, wb, tf, tb, xhalo, chalo, ahalo, dhalo, act, dpre, cots, acts,
     terms, core_in, half, rows_in, plane, z_in, own, final, send_sem, recv_sem,
 ):
     nf, strip, width, chans = x_ref.shape
@@ -127,82 +134,100 @@
     def _():
         c_prev.start()
 
+    assert width % 32 == 0
+
+    def pair(n):
+        return lax.div(n, 2), lax.rem(n, 2)
+
     def put_cots(first, src):
-        for f in range(nf):
-            for h in range(strip):
-                rows = pl.ds(first + f * width, width)
-                high, low = split(src[f, h])
-                cots[0, h, rows, :] = high
-                cots[1, h, rows, :] = low
+        def one(n):
+            h, f = pair(n)
+            high, low = split(src[f, h])
+            rows = frame_rows(first + f, width)
+            cots[0, h, rows, :] = high
+            cots[1, h, rows, :] = low
+
+        each(strip * nf, one)
+
+    def conv(src, weight, dst, flip):
+        dst[...] = jnp.zeros(dst.shape, F32)
+
+        def one(i):
+            rows = src[:, pl.ds(2 - i if flip else i, strip)]
+            dst[...] += product(rows.reshape(2 * strip * wide, three), weight[i])
+
+        each(3, one)
+
+    def temporal(src, weight, dst, flip):
+        dst[...] = jnp.zeros(dst.shape, F32)
+
+        def one(k):
+            rows = src[:, :, frame_rows(2 - k if flip else k, width, nf), :]
+            dst[...] += product(rows.reshape(2 * strip * wide, chans), weight[k])
+
+        each(3, one)
 
     loads[0].wait()
-    for h in range(strip):
-        put_row(xs, h + 1, [x_ref[f, h] for f in range(nf)])
+
+    def x_row(n):
+        h, f = pair(n)
+        put_row(xs, h + 1, f, x_ref[f, h])
+
+    each(strip * nf, x_row)
     loads[1].wait()
     put_cots(0, cot_ref)
     loads[2].wait()
-    for k in range(3):
+
+    def t_weights(k):
         put_weight(tb, k, tw_ref[k].T)
+        put_weight(tf, k, tw_ref[k])
+
+    each(3, t_weights)
     loads[3].wait()
-    for i in range(3):
-        put_weight(wf, i, sw_ref[i].reshape(three, chans))
-
-    def conv(src, row, count, weight, i):
-        return product(src[:, row : row + count].reshape(2 * count * wide, three), weight[i])
-
-    middle = conv(xs, 1, 2, wf, 1)
-    pre = [middle[:wide] + conv(xs, 2, 1, wf, 2), middle[wide:] + conv(xs, 1, 1, wf, 0)]
-
-    def temporal(src, shift, weight, k):
-        rows = pl.ds(shift * width, wide)
-        return product(src[:, :, rows, :].reshape(2 * strip * wide, chans), weight[k])
-
-    dact = temporal(cots, 0, tb, 0)
+    each(3, lambda i: put_weight(wf, i, sw_ref[i].reshape(three, chans)))
     receive(c_prev, has_next)
-    put_cots(wide, chalo)
-    dact = dact + temporal(cots, 1, tb, 1) + temporal(cots, 2, tb, 2)
-
+    put_cots(nf, chalo)
+    temporal(cots, tb, dact, False)
     receive(x_down, has_up)
-    put_row(xs, 0, [xhalo[0, f] for f in range(nf)])
     receive(x_up, has_down)
-    put_row(xs, 3, [xhalo[1, f] for f in range(nf)])
-    pre = [pre[0] + conv(xs, 0, 1, wf, 0), pre[1] + conv(xs, 3, 1, wf, 2)]
-
-    both_act, both_dpre = [], []
-    for h in range(strip):
-        sig = 1.0 / (1.0 + jnp.exp(-pre[h]))
-        act_h = pre[h] * sig
-        act[h] = act_h
-        dpre_h = dact[h * wide : (h + 1) * wide] * sig * (1.0 + pre[h] * (1.0 - sig))
-        dpre[h] = dpre_h
-        both_act.append(act_h)
-        both_dpre.append(dpre_h)
+
+    def x_edge(n):
+        side, f = pair(n)
+        put_row(xs, side * (strip + 1), f, xhalo[side, f])
+
+    each(2 * nf, x_edge)
+    conv(xs, wf, pre, False)
+
+    def gates(h):
+        rows = frame_rows(h, wide)
+        value = pre[rows]
+        sig = 1.0 / (1.0 + jnp.exp(-value))
+        act[h] = value * sig
+        dpre[h] = dact[rows] * sig * (1.0 + value * (1.0 - sig))
+
+    each(strip, gates)
 
     @pl.when(has_next)
     def _():
         a_next.start()
 
-    def stack(strips):
-        return jnp.concatenate(split(jnp.concatenate(strips, axis=0).T), axis=0)
-
-    def put_term(tap, value):
-        g, place = divmod(tap, 2 * PER_CORE)
-        terms[g, place // PER_CORE, place % PER_CORE] = value
-
-    act_t = stack(both_act)
-    for k in range(3):
-        rows = pl.ds(k * width, wide)
-        both = [cots[p, :, rows, :].reshape(strip * wide, chans) for p in range(2)]
-        put_term(k, product(act_t, jnp.concatenate(both, axis=1)).T)
-    dpre_t = stack(both_dpre)
-
-    def spatial_terms(i, first):
-        both = [xs[p, i : i + strip].reshape(strip * wide, three) for p in range(2)]
-        term = product(dpre_t, jnp.concatenate(both, axis=1))
+    for dst, src in ((act_t, act), (dpre_t, dpre)):
+        high, low = split(src[...].reshape(strip * wide, chans).T)
+        dst[:chans] = high
+        dst[chans:] = low
+
+    def temporal_terms(k):
+        both = [cots[p, :, frame_rows(k, width, nf), :].reshape(strip * wide, chans) for p in range(2)]
+        terms[k] = product(act_t[...], jnp.concatenate(both, axis=1)).T
+
+    def spatial_terms(i):
+        both = [xs[p, pl.ds(i, strip)].reshape(strip * wide, three) for p in range(2)]
+        term = product(dpre_t[...], jnp.concatenate(both, axis=1))
         for j in range(3):
-            put_term(first + j, term[:, j * chans : (j + 1) * chans])
-
-    spatial_terms(1, 3)
+            terms[3 * i + 3 + j] = term[:, j * chans : (j + 1) * chans]
+
+    each(3, temporal_terms)
+    each(3, spatial_terms)
     to_core = [None] * GROUPS
     to_rows = [None] * GROUPS
     to_z = [None] * GROUPS
@@ -210,11 +235,11 @@
     back = [None] * GROUPS
 
     def start_core(g):
-        to_core[g] = send(terms.at[g, 1 - core], core_in.at[g], frames=other)
+        to_core[g] = send(terms.at[pl.ds((2 * g + 1 - core) * PER_CORE, PER_CORE)], core_in.at[g], frames=other)
 
     def start_rows(g):
         to_core[g].wait_recv()
-        half[g] = terms[g, core] + core_in[g]
+        half[g] = terms[pl.ds((2 * g + core) * PER_CORE, PER_CORE)] + core_in[g]
         to_rows[g] = []
         for o in range(1, nrd):
             target = lax.rem(ro + o, nrd)
@@ -260,14 +285,14 @@
         gr_ref[g] = final[g]
 
     def put_acts(first, src):
-        for h in range(strip):
+        def one(h):
             high, low = split(src[h])
             acts[0, h, pl.ds(first, wide), :] = high
             acts[1, h, pl.ds(first, wide), :] = low
 
+        each(strip, one)
+
     start_core(0)
-    spatial_terms(0, 6)
-    spatial_terms(2, 9)
     start_core(1)
     start_rows(0)
     start_rows(1)
@@ -280,38 +305,44 @@
     def _():
         d_down.start()
 
-    for k in range(3):
-        put_weight(tf, k, tw_ref[k])
     put_acts(wide, act)
-    mixed = temporal(acts, 2, tf, 0)
     receive(a_next, has_prev)
     put_acts(0, ahalo)
-    mixed = mixed + temporal(acts, 1, tf, 1) + temporal(acts, 0, tf, 2)
-    for h in range(strip):
-        for f in range(nf):
-            at = h * wide + f * width
-            mix_ref[f, h] = x_ref[f, h] + mixed[at : at + width]
+    temporal(acts, tf, pre, True)
+
+    def out_row(n):
+        h, f = pair(n)
+        mix_ref[f, h] = x_ref[f, h] + pre[frame_rows(n, width)]
+
+    each(strip * nf, out_row)
     start_z(0)
-    for h in range(strip):
-        put_row(ds, h + 1, [dpre[h, pl.ds(f * width, width)] for f in range(nf)])
+
+    def d_row(n):
+        h, f = pair(n)
+        put_row(ds, h + 1, f, dpre[h, frame_rows(f, width)])
+
+    each(strip * nf, d_row)
     start_z(1)
     start_around(0)
-    for i in range(3):
-        put_weight(wb, i, jnp.concatenate([sw_ref[i, 2 - b].T for b in range(3)], axis=0))
+    each(3, lambda i: put_weight(wb, i, jnp.concatenate([sw_ref[i, 2 - b].T for b in range(3)], axis=0)))
     start_around(1)
     start_back(0)
-    middle = conv(ds, 1, 2, wb, 1)
-    grad = [middle[:wide] + conv(ds, 2, 1, wb, 0), middle[wide:] + conv(ds, 1, 1, wb, 2)]
     start_back(1)
     receive(d_down, has_up)
-    put_row(ds, 0, [dhalo[0, pl.ds(f * width, width)] for f in range(nf)])
     receive(d_up, has_down)
-    put_row(ds, 3, [dhalo[1, pl.ds(f * width, width)] for f in range(nf)])
-    grad = [grad[0] + conv(ds, 0, 1, wb, 2), grad[1] + conv(ds, 3, 1, wb, 0)]
-    for h in range(strip):
-        for f in range(nf):
-            at = f * width
-            gi_ref[f, h] = cot_ref[f, h] + grad[h][at : at + width]
+
+    def d_edge(n):
+        side, f = pair(n)
+        put_row(ds, side * (strip + 1), f, dhalo[side, frame_rows(f, width)])
+
+    each(2 * nf, d_edge)
+    conv(ds, wb, pre, True)
+
+    def grad_row(n):
+        h, f = pair(n)
+        gi_ref[f, h] = cot_ref[f, h] + pre[frame_rows(n, width)]
+
+    each(strip * nf, grad_row)
     for g in range(GROUPS):
         finish(g)
 
@@ -329,8 +360,7 @@
     for tap in range(12):
         g, place = divmod(tap, 2 * PER_CORE)
         src = gr_ref.at[g, place // PER_CORE, pl.ds(place % PER_CORE * share, share)]
-        i = (1, 0, 2)[tap // 3 - 1]
-        pairs.append((src, temporal_ref.at[tap] if tap < 3 else spatial_ref.at[i, tap % 3]))
+        pairs.append((src, temporal_ref.at[tap] if tap < 3 else spatial_ref.at[tap // 3 - 1, tap % 3]))
     copies = [pltpu.make_async_copy(src, dst, sem.at[n]) for n, (src, dst) in enumerate(pairs)]
     for copy in copies:
         copy.start()
@@ -361,6 +391,10 @@
         scratch_shapes=[
             *(pltpu.VMEM(a.shape, F32) for a in operands),
             pltpu.SemaphoreType.DMA((4,)),
+            pltpu.VMEM((strip * wide, chans), F32),
+            pltpu.VMEM((strip * wide, chans), F32),
+            pltpu.VMEM((2 * chans, strip * wide), BF16),
+            pltpu.VMEM((2 * chans, strip * wide), BF16),
             pltpu.VMEM((2, strip + 2, wide, three), BF16),
             pltpu.VMEM((2, strip + 2, wide, three), BF16),
             pltpu.VMEM((3, three, 2 * chans), BF16),
@@ -375,7 +409,7 @@
             pltpu.VMEM((strip, wide, chans), F32),
             pltpu.VMEM((2, strip, 2 * wide, chans), BF16),
             pltpu.VMEM((2, strip, 2 * wide, chans), BF16),
-            pltpu.VMEM((GROUPS, 2, PER_CORE, chans, chans), F32),
+            pltpu.VMEM((12, chans, chans), F32),
             pltpu.VMEM((GROUPS, PER_CORE, chans, chans), F32),
             pltpu.VMEM((GROUPS, PER_CORE, chans, chans), F32),
             pltpu.VMEM((GROUPS, nrd - 1, PER_CORE, share, chans), F32),

time: 32 us -> 34.6 us (1.081)
  Pallas kernels: 31.2 us -> 33.8 us
    pallas_call x1, Pallas kernels: 30.3 us -> 32.9 us  [per_device(): pl.pallas_call(functools.partial(kernel, nfd, nrd, share, piece, factor),...]
where the time goes in v9:
time: 34.6 us; the launch traced here: 34.5 us
  Pallas kernels  33.8 us (98%)
  between operations  0.64 us (2%)
    pallas_call x1, Pallas kernels, per_device(): pl.pallas_call(functools.partial(kernel, nfd, nrd, share, piece, factor),...  32.9 us
    pallas_call x1, Pallas kernels, per_device(): pl.pallas_call(functools.partial(write, share), out_shape=(jax.ShapeDtype...  0.92 us

profile of v9, /device:TPU:0, one launch (start us, length us, event | category | flops | bytes accessed | tf_op | source)
XLA Modules:
  0.0 34.5 jit_solution(11783739470288574818)
XLA Ops:
  0.6 32.9 %shard_map.75 = (f32[2,2,96,128]{3,2,1,0:T(8,128)S(1)}, f32[2,2,96,128]{3,2,1,0:T(8,128)S(1)}, f32[2,2,96,128]{3,2,1,0:T(8,128)S(1)}) custom-call(f32[2,2,96,128]{3,2,1,0:T(8,128)} %x_hbm.1, f32[3,3,128,128]{3,2,1,0:T(8,128)} %sw_hbm.1, f32[3,128,128]{2,1,0:T(8,128)} %tw_hbm.1, f32[2,2,96,128]{3,2,1,0:T(8,128)} %cot_hbm.1), custom_call_target="tpu_custom_call" | custom-call | flops 1400000000 | bytes 2000000 | tf_op jit(solution)/shard_map/pallas_call | solution.py:382
  33.6 0.9 %shard_map.76 = (f32[2,2,96,128]{3,2,1,0:T(8,128)}, f32[2,2,96,128]{3,2,1,0:T(8,128)}, f32[3,3,32,128]{3,2,1,0:T(8,128)}, f32[3,32,128]{2,1,0:T(8,128)}) custom-call(f32[2,2,96,128]{3,2,1,0:T(8,128)S(1)} %get-tuple-element.11.mix_ref, f32[2,2,96,128]{3,2,1,0:T(8,128)S(1)} %get-tuple-element.12.gi_ref, f32[2,2,96,128]{3,2,1,0:T(8,128)S(1)} %get-tuple-element.13.gr_ref), custom_call_target="tpu_custom_call" | custom-call | bytes 1200000 | tf_op jit(solution)/shard_map/pallas_call | solution.py:428
